TPU v7x, 256 devices: a whole 4x4x8 slice. The times are simulated.
256 devices in a mesh: row: 8 (over y_hi, x), col: 8 (over z), head: 4 (over y_lo, core).
Axes of the slice: x: 4, y: 4 (y_hi: 2, y_lo: 2; y = y_hi * 2 + y_lo), z: 8, core: 2. Of those that a mesh axis runs over, the one named last changes fastest.
Arguments:
- queries: bfloat16 [4, 32, 320, 1024], P('head', None, 'row', 'col'), may hold values from -6.5 to 6.5
- key_vectors: bfloat16 [4, 32, 320, 1024], P('head', None, 'row', 'col'), may hold values from -6.5 to 6.5
- value_vectors: bfloat16 [4, 32, 320, 1024], P('head', None, 'row', 'col'), may hold values from -6 to 6
- gate_logits: bfloat16 [4, 32, 320, 1024], P('head', None, 'row', 'col'), may hold values from -6 to 6
- cotangent: bfloat16 [4, 32, 320, 1024], P('head', None, 'row', 'col'), may hold values from -24 to 24
- pair_normed: bfloat16 [128, 1024, 1024], P('head', 'row', 'col'), may hold values from -6 to 6
- bias_weight: bfloat16 [128, 4], P('head'), may hold values from -0.75 to 0.75
- chain_lengths: int32 [8], replicated, may hold values from 51 to 128, as said below
Outputs:
- query_grad: bfloat16 [4, 32, 320, 1024], P('head', None, 'row', 'col')
- key_grad: bfloat16 [4, 32, 320, 1024], P('head', None, 'row', 'col')
- value_grad: bfloat16 [4, 32, 320, 1024], P('head', None, 'row', 'col')
- gate_grad: bfloat16 [4, 32, 320, 1024], P('head', None, 'row', 'col')
- pair_grad: bfloat16 [128, 1024, 1024], P('head', 'row', 'col')
Inputs may be any that keep to these rules, and one draw needn't show every extreme that they name: `chain_lengths`: every chain has at least one token; positions from the sum of the lengths on are padding.
All inputs are finite; a program needn't handle non-finite values.
Results may differ from a plain program's by a relative error of at most 0.027.
Values may be sent and summed in bfloat16 or wider, within the bound.
No kernel may reach another device: no remote copies, remote signals or barrier semaphores. Data moves between devices by JAX's collectives and lax.ppermute only.
A program may use at most 128 MiB of HBM per device.

v0:
```python
import functools
import math

import jax
import jax.numpy as jnp
from jax import lax
from jax.experimental import pallas as pl
from jax.experimental.pallas import tpu as pltpu
from jax.sharding import PartitionSpec as P

HEADS = 4
DIM = 32
BLK = 128
SCALE = DIM**-0.5
LOG2E = math.log2(math.e)
BF = jnp.bfloat16
F32 = jnp.float32
NT = (((1,), (1,)), ((), ()))
NEG = -1e9


def split_kernel(q_ref, k_ref, v_ref, g_ref, c_ref, x_ref, buf):
    cols, per = x_ref.shape[:2]
    rows = q_ref.shape[2]
    ag = (c_ref[0].astype(F32) * jax.nn.sigmoid(g_ref[0].astype(F32))).astype(BF)
    for a, value in enumerate((q_ref[0], k_ref[0], v_ref[0], ag)):
        buf[a] = value.astype(F32).reshape(DIM * rows, BLK)
    for dest in range(cols):
        for r in range(per):
            for a in range(4):
                part = buf[a, pl.ds(r * cols + dest, DIM, rows)].astype(BF)
                x_ref[dest, r, a] = part


def merge_kernel(y_ref, z_ref, g_ref, c_ref, dq_ref, dk_ref, dv_ref, dg_ref, buf):
    cols, per = y_ref.shape[:2]
    rows = dq_ref.shape[2]
    for src in range(cols):
        for r in range(per):
            for a in range(4):
                part = z_ref[src, r, a - 1] if a in (1, 2) else y_ref[src, r, a // 3]
                buf[a, pl.ds(r * cols + src, DIM, rows)] = part.astype(F32)
    for a, out in enumerate((dq_ref, dk_ref, dv_ref)):
        out[0] = buf[a].reshape(DIM, rows, BLK).astype(BF)
    gate = jax.nn.sigmoid(g_ref[0].astype(F32))
    attended = buf[3].reshape(DIM, rows, BLK)
    dg_ref[0] = (c_ref[0].astype(F32) * attended * gate * (1.0 - gate)).astype(BF)


def attend_kernel(ts, first, last, extra, *refs):
    refs = list(refs)
    take = lambda n: [refs.pop(0) for _ in range(n)]
    meta_ref, x_ref = take(2)
    b_refs = take(len(ts))
    if first:
        ka_in = vta_in = acc_in = y_in = None
    else:
        ka_in, vta_in, acc_in, y_in = take(4)
    r_refs = take(extra)
    (y_ref,) = take(1)
    z_ref = take(1)[0] if last else None
    db_refs = take(len(ts))
    if last:
        ka_out = vta_out = None
        acc_out = None
    else:
        ka_out, vta_out, acc_out = take(3)
    ka, vta, va, kk, s_ref, p_ref, acc, dbacc = refs
    cols = x_ref.shape[0]
    row = pl.program_id(0)
    count = meta_ref[0]
    place = lambda s: lax.rem(meta_ref[9] - s + cols, cols)

    @pl.when(row == 0)
    def _():
        dbacc[...] = jnp.zeros_like(dbacc)

    ones16 = jnp.ones((16, BLK), BF)
    zeros48 = jnp.zeros((48, BLK), BF)
    lane = lax.broadcasted_iota(jnp.int32, (16, BLK), 1)
    for s in range(cols):
        at = pl.ds(s * BLK, BLK)
        key = x_ref[s, 0, 1]
        val = x_ref[s, 0, 2]
        if first:
            mask = jnp.where(s * BLK + lane < count, 0.0, NEG).astype(BF)
            ka[at, :] = jnp.concatenate([key, key, mask, zeros48], 0).T
            vta[at, :] = jnp.concatenate([val, val, ones16, zeros48], 0).T
        va[0:DIM, at] = val
        va[DIM : DIM + 16, at] = ones16
        kk[:, at] = key
    if first:
        acc[...] = jnp.zeros_like(acc)
        ka_use, vta_use = ka, vta
    else:
        acc[...] = acc_in[0]
        y_ref[...] = y_in[...]
        ka_use, vta_use = ka_in.at[0], vta_in.at[0]
    if not last:
        ka_out[0] = ka_use[...]
        vta_out[0] = vta_use[...]
    sub = lax.broadcasted_iota(jnp.int32, (16, 2 * BLK), 0)
    unit = jnp.where(sub == 0, 1.0, 0.0).astype(BF)
    zero48 = jnp.zeros((48, 2 * BLK), BF)
    zero64 = jnp.zeros((64, 2 * BLK), BF)
    zero32 = jnp.zeros((32, 2 * BLK), BF)

    def scores(n, t, steps):
        b_ref = b_refs[n]
        j0 = meta_ref[1 + 2 * t]
        j1 = meta_ref[2 + 2 * t]
        q = jnp.concatenate([x_ref[j0, 0, 0], x_ref[j1, 0, 0]], 1)
        qs = q.astype(F32) * (SCALE * LOG2E)
        qhi = qs.astype(BF)
        qlo = (qs - qhi.astype(F32)).astype(BF)
        qa = jnp.concatenate([qhi, qlo, unit, zero48], 0)
        top = None
        for kb in range(steps):
            at = pl.ds(kb * 2 * BLK, 2 * BLK)
            s = jnp.dot(ka_use[at, :], qa, preferred_element_type=F32)
            bias = jnp.concatenate(
                [
                    jnp.concatenate([b_ref[0, place(2 * kb + e)], b_ref[1, place(2 * kb + e)]], 1)
                    for e in range(2)
                ],
                0,
            )
            s = s + bias
            s_ref[n, at, :] = s
            m = jnp.max(s, axis=0, keepdims=True)
            top = m if top is None else jnp.maximum(top, m)
        return j0, j1, q, top

    def weights(n, top, steps):
        o = None
        for kb in range(steps):
            at = pl.ds(kb * 2 * BLK, 2 * BLK)
            p = jnp.exp2(s_ref[n, at, :] - top)
            s_ref[n, at, :] = p
            pb = p.astype(BF)
            p_ref[n, at, :] = pb
            part = jnp.dot(va[:, at], pb, preferred_element_type=F32)
            o = part if o is None else o + part
        return o

    def middle(n, j0, j1, q, o):
        ag = jnp.concatenate([x_ref[j0, 0, 3], x_ref[j1, 0, 3]], 1).astype(F32)
        inv = 1.0 / o[DIM : DIM + 1]
        att = o[:DIM] * inv
        delta = jnp.sum(ag * att, axis=0, keepdims=True) * inv
        do = ag * inv
        dohi = do.astype(BF)
        dolo = (do - dohi.astype(F32)).astype(BF)
        d1 = delta.astype(BF).astype(F32)
        d2 = (delta - d1).astype(BF).astype(F32)
        d3 = delta - d1 - d2
        drow = jnp.where(sub == 0, -d1, jnp.where(sub == 1, -d2, jnp.where(sub == 2, -d3, 0.0)))
        doa = jnp.concatenate([dohi, dolo, drow.astype(BF), zero48], 0)
        w = jnp.concatenate(
            [
                jnp.concatenate([dohi, dolo, zero64], 0),
                jnp.concatenate([zero64, q, zero32], 0),
            ],
            1,
        )
        attb = att.astype(BF)
        y_ref[j0, 0, 1] = attb[:, :BLK]
        y_ref[j1, 0, 1] = attb[:, BLK:]
        return doa, w

    def gradients(n, kb, doa):
        at = pl.ds(kb * 2 * BLK, 2 * BLK)
        dp = jnp.dot(vta_use[at, :], doa, preferred_element_type=F32)
        ds = s_ref[n, at, :] * dp
        dsb = ds.astype(BF)
        for e in range(2):
            part = ds[e * BLK : (e + 1) * BLK]
            dbacc[n, 0, place(2 * kb + e)] += part[:, :BLK]
            dbacc[n, 1, place(2 * kb + e)] += part[:, BLK:]
        both = jnp.concatenate([p_ref[n, at, :], dsb], 1)
        return jnp.dot(kk[:, at], dsb, preferred_element_type=F32), both

    def chunks(some, steps):
        first_stage = [scores(n, ts[n], steps) for n in some]
        outs = [weights(n, f[3], steps) for n, f in zip(some, first_stage)]
        mids = [middle(n, f[0], f[1], f[2], o) for n, f, o in zip(some, first_stage, outs)]
        dqs = [None] * len(some)
        for kb in range(steps):
            at = pl.ds(kb * 2 * BLK, 2 * BLK)
            terms = []
            for i, n in enumerate(some):
                part, both = gradients(n, kb, mids[i][0])
                dqs[i] = part if dqs[i] is None else dqs[i] + part
                terms.append(lax.dot_general(both, mids[i][1], NT, preferred_element_type=F32))
            acc[at, :] += sum(terms[1:], terms[0])
        for f, dq in zip(first_stage, dqs):
            dq = (dq * SCALE).astype(BF)
            y_ref[f[0], 0, 0] = dq[:, :BLK]
            y_ref[f[1], 0, 0] = dq[:, BLK:]

    def live(steps, low, high):
        @pl.when(jnp.logical_and(count > low, count <= high))
        def _():
            for start in range(0, len(ts), 2):
                chunks(range(start, min(start + 2, len(ts))), steps)

    full = cols // 2
    live(full, (full - 1) * 2 * BLK, full * 2 * BLK)
    live(full - 1, (full - 2) * 2 * BLK, (full - 1) * 2 * BLK)
    live(full - 2, 0, (full - 2) * 2 * BLK)

    if last:
        for s in range(cols):
            a = acc[s * BLK : (s + 1) * BLK, :].T
            z_ref[s, 0, 1] = (a[0:DIM] + a[DIM : 2 * DIM]).astype(BF)
            z_ref[s, 0, 0] = (a[2 * DIM : 3 * DIM] * SCALE).astype(BF)
    else:
        acc_out[0] = acc[...]

    @pl.when(row == pl.num_programs(0) - 1)
    def _():
        for n in range(len(ts)):
            total = dbacc[n]
            if n == len(ts) - 1:
                for r_ref in r_refs:
                    total = total + r_ref[...].astype(F32)
            db_refs[n][...] = total.astype(db_refs[n].dtype)


def attend(meta, x, biases, ts, state=None, last=False, extra=()):
    first = state is None
    cols, rows = x.shape[:2]
    wide = cols * BLK
    per_row = lambda n: pl.BlockSpec((cols, 1, n, DIM, BLK), lambda r: (0, r, 0, 0, 0))
    pairs = jax.ShapeDtypeStruct((cols, rows, 2, DIM, BLK), BF)
    tile = pl.BlockSpec((2, cols, BLK, BLK), lambda r: (0, 0, 0, 0))
    flat = pl.BlockSpec((1, wide, BLK), lambda r: (r, 0, 0))
    tile_shape = (2, cols, BLK, BLK)
    flat_shape = (rows, wide, BLK)
    in_specs = [pl.BlockSpec(memory_space=pltpu.SMEM), per_row(4)] + [tile] * len(ts)
    operands = [meta, x] + [biases[t] for t in ts]
    if not first:
        in_specs += [flat, flat, flat, per_row(2)]
        operands += list(state)
    in_specs += [tile] * len(extra)
    operands += list(extra)
    out_specs = [per_row(2)] * (2 if last else 1) + [tile] * len(ts)
    out_shape = [pairs] * (2 if last else 1)
    out_shape += [jax.ShapeDtypeStruct(tile_shape, F32 if last else BF)] * len(ts)
    if not last:
        out_specs += [flat] * 3
        out_shape += [jax.ShapeDtypeStruct(flat_shape, dt) for dt in (BF, BF, F32)]
    outs = pl.pallas_call(
        functools.partial(attend_kernel, ts, first, last, len(extra)),
        grid=(rows,),
        in_specs=in_specs,
        out_specs=out_specs,
        out_shape=out_shape,
        scratch_shapes=[
            pltpu.VMEM((wide, BLK), BF),
            pltpu.VMEM((wide, BLK), BF),
            pltpu.VMEM((DIM + 16, wide), BF),
            pltpu.VMEM((DIM, wide), BF),
            pltpu.VMEM((len(ts), wide, 2 * BLK), F32),
            pltpu.VMEM((len(ts), wide, 2 * BLK), BF),
            pltpu.VMEM((wide, BLK), F32),
            pltpu.VMEM((len(ts),) + tile_shape, F32),
        ],
        compiler_params=pltpu.CompilerParams(vmem_limit_bytes=32 * 1024 * 1024),
        cost_estimate=pl.CostEstimate(
            flops=len(ts) * 2_000_000_000, bytes_accessed=8_000_000, transcendentals=0
        ),
    )(*operands)
    if last:
        return *outs[:2], dict(zip(ts, outs[2:])), None
    dbs, rest = outs[1 : 1 + len(ts)], outs[1 + len(ts) :]
    return outs[0], dict(zip(ts, dbs)), (*rest, outs[0])


VMEM_SPEC = pl.BlockSpec(memory_space=pltpu.VMEM)


def split(q, k, v, g, c, cols):
    rows = q.shape[2]
    return pl.pallas_call(
        split_kernel,
        in_specs=[VMEM_SPEC] * 5,
        out_specs=VMEM_SPEC,
        out_shape=jax.ShapeDtypeStruct((cols, rows // cols, 4, DIM, BLK), BF),
        scratch_shapes=[pltpu.VMEM((4, DIM * rows, BLK), F32)],
        compiler_params=pltpu.CompilerParams(vmem_limit_bytes=24 * 1024 * 1024),
    )(q, k, v, g, c)


def merge(y, z, g, c):
    rows = g.shape[2]
    return pl.pallas_call(
        merge_kernel,
        in_specs=[VMEM_SPEC] * 4,
        out_specs=[VMEM_SPEC] * 4,
        out_shape=[jax.ShapeDtypeStruct(g.shape, BF)] * 4,
        scratch_shapes=[pltpu.VMEM((4, DIM * rows, BLK), F32)],
        compiler_params=pltpu.CompilerParams(vmem_limit_bytes=24 * 1024 * 1024),
    )(y, z, g, c)


def shift(x, axis, n, by):
    return lax.ppermute(x, axis, [(i, (i + by) % n) for i in range(n)])


def shift_x(x, by):
    return lax.ppermute(x, "row", [(r, r // 4 * 4 + (r + by) % 4) for r in range(8)])


def swap_y(x):
    return lax.ppermute(x, "row", [(r, (r + 4) % 8) for r in range(8)])


def gather_z(own, cols):
    far = jnp.stack([own, shift(own, "col", cols, 3), shift(own, "col", cols, -3)])
    low = shift(far, "col", cols, 1)
    high = shift(far[:2], "col", cols, -1)
    return jnp.stack([own, low[0], high[1], far[1], low[1], far[2], low[2], high[0]])


def reduce_z(strip, cols, after):
    part = strip.astype(BF)
    low = shift(jnp.stack([part[1], part[4], part[6]]), "col", cols, -1).astype(F32)
    high = shift(jnp.stack([part[7], part[2]]), "col", cols, 1).astype(F32)
    low, high, after = lax.optimization_barrier((low, high, after))
    left = shift((strip[3] + low[1] + high[1]).astype(BF), "col", cols, -3).astype(F32)
    right = shift((strip[5] + low[2]).astype(BF), "col", cols, 3).astype(F32)
    return strip[0] + low[0] + high[0] + left + right, after


def body(q, k, v, g, c, pair, weight, lengths):
    cols = lax.axis_size("col")
    col = lax.axis_index("col")
    row = lax.axis_index("row")
    head = lax.axis_index("head")
    count = jnp.sum(lengths)
    away = jnp.arange(8)
    block = jnp.remainder(row // 4 + away % 2, 2) * 4 + jnp.remainder(row - away // 2, 4)
    meta = jnp.concatenate([count[None], block, col[None]]).astype(jnp.int32)

    partial = jnp.dot(
        weight.T, pair.reshape(pair.shape[0], BLK * BLK), preferred_element_type=F32
    ).reshape(HEADS, BLK, BLK)
    own = lax.dynamic_index_in_dim(partial, head, 0, keepdims=False)
    for s in range(1, HEADS):
        give = lax.dynamic_index_in_dim(
            partial, jnp.remainder(head + s, HEADS), 0, keepdims=False
        )
        own = own + shift(give, "head", HEADS, s)
    own = (own.T * LOG2E).astype(jnp.float16)

    x = split(q, k, v, g, c, cols)
    along_z = gather_z(own, cols)
    x, along_z = lax.optimization_barrier((x, along_z))
    x = lax.all_to_all(x, "col", 0, 0)
    along_y = jnp.stack([along_z, swap_y(along_z)])
    raw = {t: shift_x(along_y, t) for t in (2, 1, 3)}

    _, db, state = attend(meta, x, {2: raw[2].astype(F32)}, (2,))
    got2 = shift_x(db[2], -2)
    raw1, raw3, state = lax.optimization_barrier((raw[1], raw[3], state))
    _, db, state = attend(meta, x, {1: raw1.astype(F32), 3: raw3.astype(F32)}, (1, 3), state)
    got1, got3 = shift_x(db[1], -1), shift_x(db[3], -3)
    y, z, db, _ = attend(meta, x, {0: along_y.astype(F32)}, (0,), state, True, (got2,))

    y = lax.all_to_all(y, "col", 0, 0)
    both = db[0] + got1.astype(F32) + got3.astype(F32)
    strip = both[0] + swap_y(both[1].astype(BF)).astype(F32)
    mine, z = reduce_z(strip, cols, z)
    z = lax.all_to_all(z, "col", 0, 0)
    dq, dk, dv, dg = merge(y, z, g, c)
    mine = mine.T
    wf = weight.astype(F32)
    every = [mine] + [shift(mine, "head", HEADS, s) for s in range(1, HEADS)]
    order = jnp.remainder(head - jnp.arange(HEADS), HEADS)
    turned = jnp.take(wf, order, axis=1)
    dpair = jnp.dot(
        turned,
        jnp.stack(every).reshape(HEADS, BLK * BLK),
        precision=lax.Precision.HIGHEST,
    )
    dpair = dpair.reshape(pair.shape).astype(BF)
    return dq, dk, dv, dg, dpair


def solution(mesh):
    spec = P("head", None, "row", "col")
    pair_spec = P("head", "row", "col")
    return jax.shard_map(
        body,
        mesh=mesh,
        in_specs=(spec,) * 5 + (pair_spec, P("head", None), P()),
        out_specs=(spec,) * 4 + (pair_spec,),
        check_vma=False,
    )
```

profile of v0, /device:TPU:8, one launch (start us, length us, event | category | flops | bytes accessed | tf_op | source)
XLA Modules:
  0.0 164.1 jit_solution(5893646929826401671)
XLA Ops:
  0.7 2.0 %fusion = f32[4,128,128]{2,0,1:T(4,128)S(1)} fusion(bf16[32,4]{0,1:T(4,128)(2,1)} %param.14, bf16[4,8,128,128]{3,2,1,0:T(8,128)(2,1)} %bitcast.93), kind=kOutput, calls=%fused_computation.3 | convolution fusion | flops 4194304 | bytes 1310976 | tf_op jit(solution)/shard_map/dot_general | solution.py:346
  3.3 2.3 %collective-permute-start.1 = (f32[128,128]{0,1:T(8,128)S(1)}, f32[128,128]{0,1:T(8,128)S(1)}, u32[]{:S(2)}, u32[]{:S(2)}) collective-permute-start(f32[128,128]{0,1:T(8,128)S(1)} %bitcast.91), channel_id=1, source_target_pairs={{0,2},{1,3},{2,0},{3,1},{4,6},{5,7},{6,4},{7,5},{8,10},{9,11},{10,... | collective-permute-start | bytes 196616 | tf_op jit(solution)/shard_map/ppermute | solution.py:308
  6.0 3.2 %collective-permute-done.1 = f32[128,128]{0,1:T(8,128)S(1)} collective-permute-done((f32[128,128]{0,1:T(8,128)S(1)}, f32[128,128]{0,1:T(8,128)S(1)}, u32[]{:S(2)}, u32[]{:S(2)}) %collective-permute-start.1) | collective-permute-done | bytes 65568 | tf_op jit(solution)/shard_map/ppermute | solution.py:308
  9.7 6.1 %collective-permute-start.4 = (f16[128,128]{1,0:T(8,128)(2,1)S(1)}, f16[128,128]{1,0:T(8,128)(2,1)S(1)}, u32[]{:S(2)}, u32[]{:S(2)}) collective-permute-start(f16[128,128]{1,0:T(8,128)(2,1)S(1)} %bitcast.78), channel_id=1, source_target_pairs={{0,20},{4,24},{8,28},{12,0},{16,4},{20,8},{24,12},{28,16},{1,21},{... | collective-permute-start | bytes 98312 | tf_op jit(solution)/shard_map/ppermute | solution.py:308
  15.9 2.0 %shard_map.119 = bf16[8,5,4,32,128]{4,3,2,1,0:T(8,128)(2,1)} custom-call(bf16[1,32,40,128]{3,2,1,0:T(8,128)(2,1)S(1)} %copy-done.6, bf16[1,32,40,128]{3,2,1,0:T(8,128)(2,1)S(1)} %copy-done.7, bf16[1,32,40,128]{3,2,1,0:T(8,128)(2,1)S(1)} %copy-done.8, bf16[1,32,40,128]{3,2,1,0:T(8,128)(2,1)S(1)} %copy-done, bf16[1,32,40,128]{3,2,1,0:T(8,128)(2,1)S(1)} %copy-done.1), custom_call_target="tpu_custom_call" | custom-call | tf_op jit(solution)/shard_map/pallas_call | solution.py:285
  17.9 4.9 %collective-permute-done.3 = f16[128,128]{1,0:T(8,128)(2,1)S(1)} collective-permute-done((f16[128,128]{1,0:T(8,128)(2,1)S(1)}, f16[128,128]{1,0:T(8,128)(2,1)S(1)}, u32[]{:S(2)}, u32[]{:S(2)}) %collective-permute-start.3) | collective-permute-done | bytes 32800 | tf_op jit(solution)/shard_map/ppermute | solution.py:308
  23.9 2.3 %collective-permute-start.6 = (f16[2,128,128]{2,1,0:T(8,128)(2,1)S(1)}, f16[2,128,128]{2,1,0:T(8,128)(2,1)S(1)}, u32[]{:S(2)}, u32[]{:S(2)}) collective-permute-start(f16[2,128,128]{2,1,0:T(8,128)(2,1)S(1)} %pad_maximum_fusion.3), channel_id=1, source_target_pairs={{0,28},{4,0},{8,4},{12,8},{16,12},{20,16},{24,20},{28,24},{1,29},{... | collective-permute-start | bytes 196616 | tf_op jit(solution)/shard_map/ppermute | solution.py:308
  26.2 2.5 %collective-permute-done.5 = f16[3,128,128]{2,1,0:T(8,128)(2,1)S(1)} collective-permute-done((f16[3,128,128]{2,1,0:T(8,128)(2,1)S(1)}, f16[3,128,128]{2,1,0:T(8,128)(2,1)S(1)}, u32[]{:S(2)}, u32[]{:S(2)}) %collective-permute-start.5) | collective-permute-done | bytes 98336 | tf_op jit(solution)/shard_map/ppermute | solution.py:308
  28.9 4.2 %all-to-all-start = ((bf16[8,5,4,32,128]{4,3,2,1,0:T(8,128)(2,1)}), bf16[8,5,4,32,128]{4,3,2,1,0:T(8,128)(2,1)S(1)}, u32[]{:S(2)}, u32[]{:S(2)}) async-start(bf16[8,5,4,32,128]{4,3,2,1,0:T(8,128)(2,1)} %shard_map.119), calls=%async_computation | async-start | bytes 2621440 | tf_op jit(solution)/shard_map/all_to_all | solution.py:360
  33.1 2.4 %collective-permute-start.7 = (f16[8,128,128]{2,1,0:T(8,128)(2,1)S(1)}, f16[8,128,128]{2,1,0:T(8,128)(2,1)S(1)}, u32[]{:S(2)}, u32[]{:S(2)}) collective-permute-start(f16[8,128,128]{2,1,0:T(8,128)(2,1)S(1)} %slice_dynamic-update-slice_fusion), channel_id=1, source_target_pairs={{0,128},{32,160},{64,192},{96,224},{128,0},{160,32},{192,64},{224,... | collective-permute-start | bytes 786440 | tf_op jit(solution)/shard_map/ppermute | solution.py:316
  35.5 5.6 %collective-permute-done.7 = f16[8,128,128]{2,1,0:T(8,128)(2,1)S(1)} collective-permute-done((f16[8,128,128]{2,1,0:T(8,128)(2,1)S(1)}, f16[8,128,128]{2,1,0:T(8,128)(2,1)S(1)}, u32[]{:S(2)}, u32[]{:S(2)}) %collective-permute-start.7) | collective-permute-done | bytes 262176 | tf_op jit(solution)/shard_map/ppermute | solution.py:316
  42.1 3.0 %collective-permute-start.10 = (f16[2,8,128,128]{3,2,1,0:T(8,128)(2,1)}, f16[2,8,128,128]{3,2,1,0:T(8,128)(2,1)}, u32[]{:S(2)}, u32[]{:S(2)}) collective-permute-start(f16[2,8,128,128]{3,2,1,0:T(8,128)(2,1)} %get-tuple-element.79), channel_id=1, source_target_pairs={{0,64},{32,96},{64,0},{96,32},{128,192},{160,224},{192,128},{224,1... | collective-permute-start | bytes 1572872 | tf_op jit(solution)/shard_map/ppermute | solution.py:312
  45.7 2.6 %collective-permute-start.9 = (f16[2,8,128,128]{3,2,1,0:T(8,128)(2,1)}, f16[2,8,128,128]{3,2,1,0:T(8,128)(2,1)}, u32[]{:S(2)}, u32[]{:S(2)}) collective-permute-start(f16[2,8,128,128]{3,2,1,0:T(8,128)(2,1)} %get-tuple-element.79), channel_id=1, source_target_pairs={{0,96},{32,0},{64,32},{96,64},{128,224},{160,128},{192,160},{224,1... | collective-permute-start | bytes 1572872 | tf_op jit(solution)/shard_map/ppermute | solution.py:312
  49.7 8.5 %collective-permute-done.10 = f16[2,8,128,128]{3,2,1,0:T(8,128)(2,1)} collective-permute-done((f16[2,8,128,128]{3,2,1,0:T(8,128)(2,1)}, f16[2,8,128,128]{3,2,1,0:T(8,128)(2,1)}, u32[]{:S(2)}, u32[]{:S(2)}) %collective-permute-start.10) | collective-permute-done | bytes 524320 | tf_op jit(solution)/shard_map/ppermute | solution.py:312
  58.2 2.1 %convert_element_type.67.refs_2_ = f32[2,8,128,128]{3,2,1,0:T(8,128)} convert(f16[2,8,128,128]{3,2,1,0:T(8,128)(2,1)} %collective-permute-done.10) | non-fusion elementwise | flops 262144 | bytes 1572864 | tf_op jit(solution)/shard_map/convert_element_type | solution.py:364
  60.3 3.5 %all-to-all-done.refs_1_ = bf16[8,5,4,32,128]{4,3,2,1,0:T(8,128)(2,1)S(1)} async-done(((bf16[8,5,4,32,128]{4,3,2,1,0:T(8,128)(2,1)}), bf16[8,5,4,32,128]{4,3,2,1,0:T(8,128)(2,1)S(1)}, u32[]{:S(2)}, u32[]{:S(2)}) %all-to-all-start) | async-done | bytes 1310752 | tf_op jit(solution)/shard_map/all_to_all | solution.py:360
  65.1 10.4 %shard_map.120 = (bf16[8,5,2,32,128]{4,3,2,1,0:T(8,128)(2,1)S(1)}, bf16[2,8,128,128]{3,2,1,0:T(8,128)(2,1)S(1)}, bf16[5,1024,128]{2,1,0:T(8,128)(2,1)S(1)}, bf16...) custom-call(s32[10]{0:T(128)S(1)} %pad_add_fusion.refs_0_, bf16[8,5,4,32,128]{4,3,2,1,0:T(8,128)(2,1)S(1)} %all-to-all-done.refs_1_, ...), custom_call_target="tpu_custom_call" | custom-call | flops 2000000000 | bytes 8000000 | tf_op jit(solution)/shard_map/pallas_call | solution.py:253
  76.6 3.1 %collective-permute-start.11 = (bf16[2,8,128,128]{3,2,1,0:T(8,128)(2,1)S(1)}, bf16[2,8,128,128]{3,2,1,0:T(8,128)(2,1)S(1)}, u32[]{:S(2)}, u32[]{:S(2)}) collective-permute-start(bf16[2,8,128,128]{3,2,1,0:T(8,128)(2,1)S(1)} %get-tuple-element.50), channel_id=1, source_target_pairs={{0,64},{32,96},{64,0},{96,32},{128,192},{160,224},{192,128},{224,1... | collective-permute-start | bytes 1572872 | tf_op jit(solution)/shard_map/ppermute | solution.py:312
  79.7 15.7 %shard_map.121 = (bf16[8,5,2,32,128]{4,3,2,1,0:T(8,128)(2,1)S(1)}, bf16[2,8,128,128]{3,2,1,0:T(8,128)(2,1)S(1)}, bf16[2,8,128,128]{3,2,1,0:T(8,128)(2,1)}, bf16[...) custom-call(s32[10]{0:T(128)S(1)} %pad_add_fusion.refs_0_, ...), custom_call_target="tpu_custom_call" | custom-call | flops 4000000000 | bytes 8000000 | tf_op jit(solution)/shard_map/pallas_call | solution.py:253
  96.1 2.7 %collective-permute-start.12 = (bf16[2,8,128,128]{3,2,1,0:T(8,128)(2,1)S(1)}, bf16[2,8,128,128]{3,2,1,0:T(8,128)(2,1)}, u32[]{:S(2)}, u32[]{:S(2)}) collective-permute-start(bf16[2,8,128,128]{3,2,1,0:T(8,128)(2,1)S(1)} %get-tuple-element.53), channel_id=1, source_target_pairs={{0,96},{32,0},{64,32},{96,64},{128,224},{160,128},{192,160},{224,1... | collective-permute-start | bytes 1572872 | tf_op jit(solution)/shard_map/ppermute | solution.py:312
  98.7 10.9 %shard_map.122 = (bf16[8,5,2,32,128]{4,3,2,1,0:T(8,128)(2,1)S(1)}, bf16[8,5,2,32,128]{4,3,2,1,0:T(8,128)(2,1)}, f32[2,8,128,128]{3,2,1,0:T(8,128)S(1)}) custom-call(s32[10]{0:T(128)S(1)} %pad_add_fusion.refs_0_, bf16[8,5,4,32,128]{4,3,2,1,0:T(8,128)(2,1)S(1)} %all-to-all-done.refs_1_, f32[2,8,128,128]{3,2,1,0:T(8,128)S(1)} %get-tuple-element.80.refs_2_, ...), custom_call_target="tpu_custom_call" | custom-call | flops 2000000000 | bytes 8000000 | tf_op jit(solution)/shard_map/pallas_call | solution.py:253
  111.5 3.7 %all-to-all-start.1 = ((bf16[8,5,2,32,128]{4,3,2,1,0:T(8,128)(2,1)}), bf16[8,5,2,32,128]{4,3,2,1,0:T(8,128)(2,1)S(1)}, u32[]{:S(2)}, u32[]{:S(2)}) async-start(bf16[8,5,2,32,128]{4,3,2,1,0:T(8,128)(2,1)} %copy-done.5), calls=%async_computation.1 | async-start | bytes 1310720 | tf_op jit(solution)/shard_map/all_to_all | solution.py:371
  116.6 2.4 %collective-permute-start.14 = (bf16[8,128,128]{2,1,0:T(8,128)(2,1)S(1)}, bf16[8,128,128]{2,1,0:T(8,128)(2,1)S(1)}, u32[]{:S(2)}, u32[]{:S(2)}) collective-permute-start(bf16[8,128,128]{2,1,0:T(8,128)(2,1)S(1)} %fusion.4), channel_id=1, source_target_pairs={{0,128},{32,160},{64,192},{96,224},{128,0},{160,32},{192,64},{224,... | collective-permute-start | bytes 786440 | tf_op jit(solution)/shard_map/ppermute | solution.py:316
  119.0 5.6 %collective-permute-done.14 = bf16[8,128,128]{2,1,0:T(8,128)(2,1)S(1)} collective-permute-done((bf16[8,128,128]{2,1,0:T(8,128)(2,1)S(1)}, bf16[8,128,128]{2,1,0:T(8,128)(2,1)S(1)}, u32[]{:S(2)}, u32[]{:S(2)}) %collective-permute-start.14) | collective-permute-done | bytes 262176 | tf_op jit(solution)/shard_map/ppermute | solution.py:316
  124.7 3.2 %collective-permute-start.15 = (bf16[3,128,128]{2,1,0:T(8,128)(2,1)S(1)}, bf16[3,128,128]{2,1,0:T(8,128)(2,1)S(1)}, u32[]{:S(2)}, u32[]{:S(2)}) collective-permute-start(bf16[3,128,128]{2,1,0:T(8,128)(2,1)S(1)} %pad_maximum_fusion.2), channel_id=1, source_target_pairs={{0,28},{4,0},{8,4},{12,8},{16,12},{20,16},{24,20},{28,24},{1,29},{... | collective-permute-start | bytes 294920 | tf_op jit(solution)/shard_map/ppermute | solution.py:308
  128.1 5.5 %collective-permute-done.16 = bf16[2,128,128]{2,1,0:T(8,128)(2,1)S(1)} collective-permute-done((bf16[2,128,128]{2,1,0:T(8,128)(2,1)S(1)}, bf16[2,128,128]{2,1,0:T(8,128)(2,1)S(1)}, u32[]{:S(2)}, u32[]{:S(2)}) %collective-permute-start.16) | collective-permute-done | bytes 65568 | tf_op jit(solution)/shard_map/ppermute | solution.py:308
  133.6 4.5 %all-to-all-start.2 = ((bf16[8,5,2,32,128]{4,3,2,1,0:T(8,128)(2,1)}), bf16[8,5,2,32,128]{4,3,2,1,0:T(8,128)(2,1)S(1)}, u32[]{:S(2)}, u32[]{:S(2)}) async-start(bf16[8,5,2,32,128]{4,3,2,1,0:T(8,128)(2,1)} %get-tuple-element.56), calls=%async_computation.2 | async-start | bytes 1310720 | tf_op jit(solution)/shard_map/all_to_all | solution.py:375
  138.2 3.9 %collective-permute-start.18 = (bf16[128,128]{1,0:T(8,128)(2,1)S(1)}, bf16[128,128]{1,0:T(8,128)(2,1)S(1)}, u32[]{:S(2)}, u32[]{:S(2)}) collective-permute-start(bf16[128,128]{1,0:T(8,128)(2,1)S(1)} %get-tuple-element.78), channel_id=1, source_target_pairs={{0,12},{4,16},{8,20},{12,24},{16,28},{20,0},{24,4},{28,8},{1,13},{... | collective-permute-start | bytes 98312 | tf_op jit(solution)/shard_map/ppermute | solution.py:308
  143.9 9.4 %collective-permute-done.18 = bf16[128,128]{1,0:T(8,128)(2,1)S(1)} collective-permute-done((bf16[128,128]{1,0:T(8,128)(2,1)S(1)}, bf16[128,128]{1,0:T(8,128)(2,1)S(1)}, u32[]{:S(2)}, u32[]{:S(2)}) %collective-permute-start.18) | collective-permute-done | bytes 32800 | tf_op jit(solution)/shard_map/ppermute | solution.py:308
  156.0 2.4 %collective-permute-done.20 = f32[128,128]{0,1:T(8,128)S(1)} collective-permute-done((f32[128,128]{0,1:T(8,128)S(1)}, f32[128,128]{0,1:T(8,128)S(1)}, u32[]{:S(2)}, u32[]{:S(2)}) %collective-permute-start.20) | collective-permute-done | bytes 65568 | tf_op jit(solution)/shard_map/ppermute | solution.py:308
  158.8 2.1 %convolution_convert_fusion = bf16[32,128,128]{2,0,1:T(8,128)(2,1)S(1)} fusion(f32[1,16384]{1,0:T(1,128)S(1)} %bitcast.85, f32[1,16384]{1,0:T(1,128)S(1)} %bitcast.86, f32[1,16384]{1,0:T(1,128)S(1)} %bitcast.87, f32[1,16384]{1,0:T(1,128)S(1)} %bitcast.84, f32[4,32]{1,0:T(4,128)S(1)} %gather_fusion, pred[4]{0:T(512)(128)(4,1)S(1)} %compare_and_fusion), kind=kOutput, calls=%fused_computation.1 | convolution fusion | flops 25886848 | bytes 1311236 | tf_op jit(solution)/shard_map/dot_general | solution.py:382
  162.2 1.9 %shard_map.123 = (bf16[1,32,40,128]{3,2,1,0:T(8,128)(2,1)}, bf16[1,32,40,128]{3,2,1,0:T(8,128)(2,1)}, bf16[1,32,40,128]{3,2,1,0:T(8,128)(2,1)}, bf16[1,32,40,128]{3,2,1,0:T(8,128)(2,1)}) custom-call(bf16[8,5,2,32,128]{4,3,2,1,0:T(8,128)(2,1)S(1)} %all-to-all-done.1.y_ref, bf16[8,5,2,32,128]{4,3,2,1,0:T(8,128)(2,1)S(1)} %all-to-all-done.2.z_ref, ...), custom_call_target="tpu_custom_call" | custom-call | tf_op jit(solution)/shard_map/pallas_call | solution.py:297
  (89 shorter events, 18.5 us)
Async XLA Ops:
  0.7 15.1 %copy-start = (bf16[1,32,40,128]{3,2,1,0:T(8,128)(2,1)S(1)}, bf16[1,32,40,128]{3,2,1,0:T(8,128)(2,1)}, u32[]{:S(2)}) copy-start(bf16[1,32,40,128]{3,2,1,0:T(8,128)(2,1)} %g_ref.3) | copy-start | bytes 983044
  0.7 15.1 %copy-start.1 = (bf16[1,32,40,128]{3,2,1,0:T(8,128)(2,1)S(1)}, bf16[1,32,40,128]{3,2,1,0:T(8,128)(2,1)}, u32[]{:S(2)}) copy-start(bf16[1,32,40,128]{3,2,1,0:T(8,128)(2,1)} %c_ref.3) | copy-start | bytes 983044
  0.7 15.1 %copy-start.6 = (bf16[1,32,40,128]{3,2,1,0:T(8,128)(2,1)S(1)}, bf16[1,32,40,128]{3,2,1,0:T(8,128)(2,1)}, u32[]{:S(2)}) copy-start(bf16[1,32,40,128]{3,2,1,0:T(8,128)(2,1)} %q_ref.1) | copy-start | bytes 983044
  0.7 15.1 %copy-start.7 = (bf16[1,32,40,128]{3,2,1,0:T(8,128)(2,1)S(1)}, bf16[1,32,40,128]{3,2,1,0:T(8,128)(2,1)}, u32[]{:S(2)}) copy-start(bf16[1,32,40,128]{3,2,1,0:T(8,128)(2,1)} %k_ref.1) | copy-start | bytes 983044
  0.7 15.1 %copy-start.8 = (bf16[1,32,40,128]{3,2,1,0:T(8,128)(2,1)S(1)}, bf16[1,32,40,128]{3,2,1,0:T(8,128)(2,1)}, u32[]{:S(2)}) copy-start(bf16[1,32,40,128]{3,2,1,0:T(8,128)(2,1)} %v_ref.1) | copy-start | bytes 983044
  3.1 2.9 %collective-permute-start.2 = (f32[128,128]{0,1:T(8,128)S(1)}, f32[128,128]{0,1:T(8,128)S(1)}, u32[]{:S(2)}, u32[]{:S(2)}) collective-permute-start(f32[128,128]{0,1:T(8,128)S(1)} %bitcast.90), channel_id=1, source_target_pairs={{0,3},{1,0},{2,1},{3,2},{4,7},{5,4},{6,5},{7,6},{8,11},{9,8},{10,9... | collective-permute-start | bytes 196616 | tf_op jit(solution)/shard_map/ppermute | solution.py:308
  3.3 6.0 %collective-permute-start.1 = (f32[128,128]{0,1:T(8,128)S(1)}, f32[128,128]{0,1:T(8,128)S(1)}, u32[]{:S(2)}, u32[]{:S(2)}) collective-permute-start(f32[128,128]{0,1:T(8,128)S(1)} %bitcast.91), channel_id=1, source_target_pairs={{0,2},{1,3},{2,0},{3,1},{4,6},{5,7},{6,4},{7,5},{8,10},{9,11},{10,... | collective-permute-start | bytes 196616 | tf_op jit(solution)/shard_map/ppermute | solution.py:308
  5.6 4.1 %collective-permute-start = (f32[128,128]{0,1:T(8,128)S(1)}, f32[128,128]{0,1:T(8,128)S(1)}, u32[]{:S(2)}, u32[]{:S(2)}) collective-permute-start(f32[128,128]{0,1:T(8,128)S(1)} %bitcast.92), channel_id=1, source_target_pairs={{0,1},{1,2},{2,3},{3,0},{4,5},{5,6},{6,7},{7,4},{8,9},{9,10},{10,1... | collective-permute-start | bytes 196616 | tf_op jit(solution)/shard_map/ppermute | solution.py:308
  9.7 8.1 %collective-permute-start.4 = (f16[128,128]{1,0:T(8,128)(2,1)S(1)}, f16[128,128]{1,0:T(8,128)(2,1)S(1)}, u32[]{:S(2)}, u32[]{:S(2)}) collective-permute-start(f16[128,128]{1,0:T(8,128)(2,1)S(1)} %bitcast.78), channel_id=1, source_target_pairs={{0,20},{4,24},{8,28},{12,0},{16,4},{20,8},{24,12},{28,16},{1,21},{... | collective-permute-start | bytes 98312 | tf_op jit(solution)/shard_map/ppermute | solution.py:308
  15.8 7.0 %collective-permute-start.3 = (f16[128,128]{1,0:T(8,128)(2,1)S(1)}, f16[128,128]{1,0:T(8,128)(2,1)S(1)}, u32[]{:S(2)}, u32[]{:S(2)}) collective-permute-start(f16[128,128]{1,0:T(8,128)(2,1)S(1)} %bitcast.79), channel_id=1, source_target_pairs={{0,12},{4,16},{8,20},{12,24},{16,28},{20,0},{24,4},{28,8},{1,13},{... | collective-permute-start | bytes 98312 | tf_op jit(solution)/shard_map/ppermute | solution.py:308
  22.8 5.9 %collective-permute-start.5 = (f16[3,128,128]{2,1,0:T(8,128)(2,1)S(1)}, f16[3,128,128]{2,1,0:T(8,128)(2,1)S(1)}, u32[]{:S(2)}, u32[]{:S(2)}) collective-permute-start(f16[3,128,128]{2,1,0:T(8,128)(2,1)S(1)} %pad_maximum_fusion.1), channel_id=1, source_target_pairs={{0,4},{4,8},{8,12},{12,16},{16,20},{20,24},{24,28},{28,0},{1,5},{5... | collective-permute-start | bytes 294920 | tf_op jit(solution)/shard_map/ppermute | solution.py:308
  23.9 4.8 %collective-permute-start.6 = (f16[2,128,128]{2,1,0:T(8,128)(2,1)S(1)}, f16[2,128,128]{2,1,0:T(8,128)(2,1)S(1)}, u32[]{:S(2)}, u32[]{:S(2)}) collective-permute-start(f16[2,128,128]{2,1,0:T(8,128)(2,1)S(1)} %pad_maximum_fusion.3), channel_id=1, source_target_pairs={{0,28},{4,0},{8,4},{12,8},{16,12},{20,16},{24,20},{28,24},{1,29},{... | collective-permute-start | bytes 196616 | tf_op jit(solution)/shard_map/ppermute | solution.py:308
  28.9 34.9 %all-to-all-start = ((bf16[8,5,4,32,128]{4,3,2,1,0:T(8,128)(2,1)}), bf16[8,5,4,32,128]{4,3,2,1,0:T(8,128)(2,1)S(1)}, u32[]{:S(2)}, u32[]{:S(2)}) async-start(bf16[8,5,4,32,128]{4,3,2,1,0:T(8,128)(2,1)} %shard_map.119), calls=%async_computation | async-start | bytes 2621440 | tf_op jit(solution)/shard_map/all_to_all | solution.py:360
  33.1 15.2 %copy-start.10 = (s32[8]{0:T(128)S(1)}, s32[8]{0:T(128)}, u32[]{:S(2)}) copy-start(s32[8]{0:T(128)} %param.15) | copy-start | bytes 100
  33.1 8.0 %collective-permute-start.7 = (f16[8,128,128]{2,1,0:T(8,128)(2,1)S(1)}, f16[8,128,128]{2,1,0:T(8,128)(2,1)S(1)}, u32[]{:S(2)}, u32[]{:S(2)}) collective-permute-start(f16[8,128,128]{2,1,0:T(8,128)(2,1)S(1)} %slice_dynamic-update-slice_fusion), channel_id=1, source_target_pairs={{0,128},{32,160},{64,192},{96,224},{128,0},{160,32},{192,64},{224,... | collective-permute-start | bytes 786440 | tf_op jit(solution)/shard_map/ppermute | solution.py:316
  42.1 16.1 %collective-permute-start.10 = (f16[2,8,128,128]{3,2,1,0:T(8,128)(2,1)}, f16[2,8,128,128]{3,2,1,0:T(8,128)(2,1)}, u32[]{:S(2)}, u32[]{:S(2)}) collective-permute-start(f16[2,8,128,128]{3,2,1,0:T(8,128)(2,1)} %get-tuple-element.79), channel_id=1, source_target_pairs={{0,64},{32,96},{64,0},{96,32},{128,192},{160,224},{192,128},{224,1... | collective-permute-start | bytes 1572872 | tf_op jit(solution)/shard_map/ppermute | solution.py:312
  45.1 30.3 %collective-permute-start.8 = (f16[2,8,128,128]{3,2,1,0:T(8,128)(2,1)}, f16[2,8,128,128]{3,2,1,0:T(8,128)(2,1)S(1)}, u32[]{:S(2)}, u32[]{:S(2)}) collective-permute-start(f16[2,8,128,128]{3,2,1,0:T(8,128)(2,1)} %get-tuple-element.79), channel_id=1, source_target_pairs={{0,32},{32,64},{64,96},{96,0},{128,160},{160,192},{192,224},{224,1... | collective-permute-start | bytes 1572872 | tf_op jit(solution)/shard_map/ppermute | solution.py:312
  45.7 29.7 %collective-permute-start.9 = (f16[2,8,128,128]{3,2,1,0:T(8,128)(2,1)}, f16[2,8,128,128]{3,2,1,0:T(8,128)(2,1)}, u32[]{:S(2)}, u32[]{:S(2)}) collective-permute-start(f16[2,8,128,128]{3,2,1,0:T(8,128)(2,1)} %get-tuple-element.79), channel_id=1, source_target_pairs={{0,96},{32,0},{64,32},{96,64},{128,224},{160,128},{192,160},{224,1... | collective-permute-start | bytes 1572872 | tf_op jit(solution)/shard_map/ppermute | solution.py:312
  76.6 22.1 %collective-permute-start.11 = (bf16[2,8,128,128]{3,2,1,0:T(8,128)(2,1)S(1)}, bf16[2,8,128,128]{3,2,1,0:T(8,128)(2,1)S(1)}, u32[]{:S(2)}, u32[]{:S(2)}) collective-permute-start(bf16[2,8,128,128]{3,2,1,0:T(8,128)(2,1)S(1)} %get-tuple-element.50), channel_id=1, source_target_pairs={{0,64},{32,96},{64,0},{96,32},{128,192},{160,224},{192,128},{224,1... | collective-permute-start | bytes 1572872 | tf_op jit(solution)/shard_map/ppermute | solution.py:312
  95.5 19.7 %collective-permute-start.13 = (bf16[2,8,128,128]{3,2,1,0:T(8,128)(2,1)}, bf16[2,8,128,128]{3,2,1,0:T(8,128)(2,1)}, u32[]{:S(2)}, u32[]{:S(2)}) collective-permute-start(bf16[2,8,128,128]{3,2,1,0:T(8,128)(2,1)} %get-tuple-element.54), channel_id=1, source_target_pairs={{0,32},{32,64},{64,96},{96,0},{128,160},{160,192},{192,224},{224,1... | collective-permute-start | bytes 1572872 | tf_op jit(solution)/shard_map/ppermute | solution.py:312
  96.1 19.1 %collective-permute-start.12 = (bf16[2,8,128,128]{3,2,1,0:T(8,128)(2,1)S(1)}, bf16[2,8,128,128]{3,2,1,0:T(8,128)(2,1)}, u32[]{:S(2)}, u32[]{:S(2)}) collective-permute-start(bf16[2,8,128,128]{3,2,1,0:T(8,128)(2,1)S(1)} %get-tuple-element.53), channel_id=1, source_target_pairs={{0,96},{32,0},{64,32},{96,64},{128,224},{160,128},{192,160},{224,1... | collective-permute-start | bytes 1572872 | tf_op jit(solution)/shard_map/ppermute | solution.py:312
  111.5 22.1 %all-to-all-start.1 = ((bf16[8,5,2,32,128]{4,3,2,1,0:T(8,128)(2,1)}), bf16[8,5,2,32,128]{4,3,2,1,0:T(8,128)(2,1)S(1)}, u32[]{:S(2)}, u32[]{:S(2)}) async-start(bf16[8,5,2,32,128]{4,3,2,1,0:T(8,128)(2,1)} %copy-done.5), calls=%async_computation.1 | async-start | bytes 1310720 | tf_op jit(solution)/shard_map/all_to_all | solution.py:371
  116.6 8.0 %collective-permute-start.14 = (bf16[8,128,128]{2,1,0:T(8,128)(2,1)S(1)}, bf16[8,128,128]{2,1,0:T(8,128)(2,1)S(1)}, u32[]{:S(2)}, u32[]{:S(2)}) collective-permute-start(bf16[8,128,128]{2,1,0:T(8,128)(2,1)S(1)} %fusion.4), channel_id=1, source_target_pairs={{0,128},{32,160},{64,192},{96,224},{128,0},{160,32},{192,64},{224,... | collective-permute-start | bytes 786440 | tf_op jit(solution)/shard_map/ppermute | solution.py:316
  124.7 18.7 %copy-start.9 = (bf16[32,4]{0,1:T(4,128)(2,1)S(1)}, bf16[32,4]{0,1:T(4,128)(2,1)}, u32[]{:S(2)}) copy-start(bf16[32,4]{0,1:T(4,128)(2,1)} %param.14) | copy-start | bytes 772
  124.7 8.8 %collective-permute-start.15 = (bf16[3,128,128]{2,1,0:T(8,128)(2,1)S(1)}, bf16[3,128,128]{2,1,0:T(8,128)(2,1)S(1)}, u32[]{:S(2)}, u32[]{:S(2)}) collective-permute-start(bf16[3,128,128]{2,1,0:T(8,128)(2,1)S(1)} %pad_maximum_fusion.2), channel_id=1, source_target_pairs={{0,28},{4,0},{8,4},{12,8},{16,12},{20,16},{24,20},{28,24},{1,29},{... | collective-permute-start | bytes 294920 | tf_op jit(solution)/shard_map/ppermute | solution.py:308
  128.0 5.5 %collective-permute-start.16 = (bf16[2,128,128]{2,1,0:T(8,128)(2,1)S(1)}, bf16[2,128,128]{2,1,0:T(8,128)(2,1)S(1)}, u32[]{:S(2)}, u32[]{:S(2)}) collective-permute-start(bf16[2,128,128]{2,1,0:T(8,128)(2,1)S(1)} %pad_maximum_fusion.4), channel_id=1, source_target_pairs={{0,4},{4,8},{8,12},{12,16},{16,20},{20,24},{24,28},{28,0},{1,5},{5... | collective-permute-start | bytes 196616 | tf_op jit(solution)/shard_map/ppermute | solution.py:308
  133.6 28.6 %all-to-all-start.2 = ((bf16[8,5,2,32,128]{4,3,2,1,0:T(8,128)(2,1)}), bf16[8,5,2,32,128]{4,3,2,1,0:T(8,128)(2,1)S(1)}, u32[]{:S(2)}, u32[]{:S(2)}) async-start(bf16[8,5,2,32,128]{4,3,2,1,0:T(8,128)(2,1)} %get-tuple-element.56), calls=%async_computation.2 | async-start | bytes 1310720 | tf_op jit(solution)/shard_map/all_to_all | solution.py:375
  138.2 15.2 %collective-permute-start.18 = (bf16[128,128]{1,0:T(8,128)(2,1)S(1)}, bf16[128,128]{1,0:T(8,128)(2,1)S(1)}, u32[]{:S(2)}, u32[]{:S(2)}) collective-permute-start(bf16[128,128]{1,0:T(8,128)(2,1)S(1)} %get-tuple-element.78), channel_id=1, source_target_pairs={{0,12},{4,16},{8,20},{12,24},{16,28},{20,0},{24,4},{28,8},{1,13},{... | collective-permute-start | bytes 98312 | tf_op jit(solution)/shard_map/ppermute | solution.py:308
  142.1 11.3 %collective-permute-start.17 = (bf16[128,128]{1,0:T(8,128)(2,1)S(1)}, bf16[128,128]{1,0:T(8,128)(2,1)S(1)}, u32[]{:S(2)}, u32[]{:S(2)}) collective-permute-start(bf16[128,128]{1,0:T(8,128)(2,1)S(1)} %get-tuple-element.77), channel_id=1, source_target_pairs={{0,20},{4,24},{8,28},{12,0},{16,4},{20,8},{24,12},{28,16},{1,21},{... | collective-permute-start | bytes 98312 | tf_op jit(solution)/shard_map/ppermute | solution.py:308
  153.4 2.6 %collective-permute-start.21 = (f32[128,128]{0,1:T(8,128)S(1)}, f32[128,128]{0,1:T(8,128)S(1)}, u32[]{:S(2)}, u32[]{:S(2)}) collective-permute-start(f32[128,128]{0,1:T(8,128)S(1)} %fusion.18), channel_id=1, source_target_pairs={{0,3},{1,0},{2,1},{3,2},{4,7},{5,4},{6,5},{7,6},{8,11},{9,8},{10,9... | collective-permute-start | bytes 196616 | tf_op jit(solution)/shard_map/ppermute | solution.py:308
  153.4 5.0 %collective-permute-start.20 = (f32[128,128]{0,1:T(8,128)S(1)}, f32[128,128]{0,1:T(8,128)S(1)}, u32[]{:S(2)}, u32[]{:S(2)}) collective-permute-start(f32[128,128]{0,1:T(8,128)S(1)} %fusion.18), channel_id=1, source_target_pairs={{0,2},{1,3},{2,0},{3,1},{4,6},{5,7},{6,4},{7,5},{8,10},{9,11},{10,... | collective-permute-start | bytes 196616 | tf_op jit(solution)/shard_map/ppermute | solution.py:308
  153.9 4.7 %collective-permute-start.19 = (f32[128,128]{0,1:T(8,128)S(1)}, f32[128,128]{0,1:T(8,128)S(1)}, u32[]{:S(2)}, u32[]{:S(2)}) collective-permute-start(f32[128,128]{0,1:T(8,128)S(1)} %fusion.18), channel_id=1, source_target_pairs={{0,1},{1,2},{2,3},{3,0},{4,5},{5,6},{6,7},{7,4},{8,9},{9,10},{10,1... | collective-permute-start | bytes 196616 | tf_op jit(solution)/shard_map/ppermute | solution.py:308
  (4 other events, 6.8 us)
where the time goes:
time: 163 us; the launch traced here: 164 us
  waiting for transfers between devices  53.4 us (33%)
  starting transfers between devices  51.2 us (31%)
  Pallas kernels  40.9 us (25%)
  other arithmetic  7.29 us (4%)
  local copies, waits for them, and re-layouts  6.15 us (4%)
  matrix products  4.09 us (3%)
    pallas_call x3, Pallas kernels, attend(): pl.pallas_call(functools.partial(attend_kernel, ts, first, last, len(extr...  37 us
    ppermute x14, waiting for transfers between devices, shift(): return lax.ppermute(x, axis, [(i, (i + by) % n) for i in range(n)])  30.2 us
    ppermute x14, starting transfers between devices, shift(): return lax.ppermute(x, axis, [(i, (i + by) % n) for i in range(n)])  21.4 us
    ppermute x6, starting transfers between devices, shift_x(): lax.ppermute(x, 'row', [(r, r // 4 * 4 + (r + by) % 4) for r in range(8)])  12.6 us
    ppermute x2, waiting for transfers between devices, swap_y(): return lax.ppermute(x, 'row', [(r, (r + 4) % 8) for r in range(8)])  11.2 us
    ppermute x6, waiting for transfers between devices, shift_x(): lax.ppermute(x, 'row', [(r, r // 4 * 4 + (r + by) % 4) for r in range(8)])  8.51 us
    ppermute x2, starting transfers between devices, swap_y(): return lax.ppermute(x, 'row', [(r, (r + 4) % 8) for r in range(8)])  4.77 us
    unnamed x29, local copies, waits for them, and re-layouts  4.59 us
  transfers between devices with their start and end apart: 25, of which 13 were waited for; matrix products, arithmetic and copies ran while one was open for 7% of the time, Pallas kernels for 24%

commit v1 on v0

--- a/solution.py
+++ b/solution.py
@@ -266,7 +266,9 @@
             pltpu.VMEM((wide, BLK), F32),
             pltpu.VMEM((len(ts),) + tile_shape, F32),
         ],
-        compiler_params=pltpu.CompilerParams(vmem_limit_bytes=32 * 1024 * 1024),
+        compiler_params=pltpu.CompilerParams(
+            vmem_limit_bytes=(18 if len(ts) > 1 else 11) * 1024 * 1024
+        ),
         cost_estimate=pl.CostEstimate(
             flops=len(ts) * 2_000_000_000, bytes_accessed=8_000_000, transcendentals=0
         ),
@@ -288,7 +290,7 @@
         out_specs=VMEM_SPEC,
         out_shape=jax.ShapeDtypeStruct((cols, rows // cols, 4, DIM, BLK), BF),
         scratch_shapes=[pltpu.VMEM((4, DIM * rows, BLK), F32)],
-        compiler_params=pltpu.CompilerParams(vmem_limit_bytes=24 * 1024 * 1024),
+        compiler_params=pltpu.CompilerParams(vmem_limit_bytes=8 * 1024 * 1024),
     )(q, k, v, g, c)
 
 
@@ -300,7 +302,7 @@
         out_specs=[VMEM_SPEC] * 4,
         out_shape=[jax.ShapeDtypeStruct(g.shape, BF)] * 4,
         scratch_shapes=[pltpu.VMEM((4, DIM * rows, BLK), F32)],
-        compiler_params=pltpu.CompilerParams(vmem_limit_bytes=24 * 1024 * 1024),
+        compiler_params=pltpu.CompilerParams(vmem_limit_bytes=8 * 1024 * 1024),
     )(y, z, g, c)
 
 
@@ -327,9 +329,9 @@
     part = strip.astype(BF)
     low = shift(jnp.stack([part[1], part[4], part[6]]), "col", cols, -1).astype(F32)
     high = shift(jnp.stack([part[7], part[2]]), "col", cols, 1).astype(F32)
-    low, high, after = lax.optimization_barrier((low, high, after))
     left = shift((strip[3] + low[1] + high[1]).astype(BF), "col", cols, -3).astype(F32)
     right = shift((strip[5] + low[2]).astype(BF), "col", cols, 3).astype(F32)
+    left, right, after = lax.optimization_barrier((left, right, after))
     return strip[0] + low[0] + high[0] + left + right, after
 
 

time: 163 us -> 158 us (0.969); the launches traced: 164 us -> 157 us
  Pallas kernels: 40.9 us -> 34.2 us
    pallas_call x3, Pallas kernels: 37 us -> 30.4 us  [attend(): pl.pallas_call(functools.partial(attend_kernel, ts, first, last, len(extr...]
    all_to_all x1, waiting for transfers between devices: 0.01 us -> 4.49 us  [body(): z = lax.all_to_all(z, 'col', 0, 0)]
    ppermute x2, waiting for transfers between devices: 11.2 us -> 7.61 us  [swap_y(): return lax.ppermute(x, 'row', [(r, (r + 4) % 8) for r in range(8)])]
    unnamed x29 -> x25, local copies, waits for them, and re-layouts: 4.59 us -> 3.4 us
  transfers between devices with their start and end apart: 25 -> 25, of which waited for: 13 -> 15; matrix products, arithmetic and copies ran while one was open for 7% -> 6% of each run, Pallas kernels for 24% -> 21%
where the time goes in v1:
time: 158 us; the launch traced here: 157 us
  waiting for transfers between devices  54.3 us (34%)
  starting transfers between devices  52.3 us (33%)
  Pallas kernels  34.2 us (22%)
  other arithmetic  6.11 us (4%)
  local copies, waits for them, and re-layouts  4.95 us (3%)
  matrix products  4.09 us (3%)
    pallas_call x3, Pallas kernels, attend(): pl.pallas_call(functools.partial(attend_kernel, ts, first, last, len(extr...  30.4 us
    ppermute x14, waiting for transfers between devices, shift(): return lax.ppermute(x, axis, [(i, (i + by) % n) for i in range(n)])  30.2 us
    ppermute x14, starting transfers between devices, shift(): return lax.ppermute(x, axis, [(i, (i + by) % n) for i in range(n)])  21.8 us
    ppermute x6, starting transfers between devices, shift_x(): lax.ppermute(x, 'row', [(r, r // 4 * 4 + (r + by) % 4) for r in range(8)])  12.7 us
    ppermute x6, waiting for transfers between devices, shift_x(): lax.ppermute(x, 'row', [(r, r // 4 * 4 + (r + by) % 4) for r in range(8)])  8.51 us
    ppermute x2, waiting for transfers between devices, swap_y(): return lax.ppermute(x, 'row', [(r, (r + 4) % 8) for r in range(8)])  7.61 us
    all_to_all x1, starting transfers between devices, body(): z = lax.all_to_all(z, 'col', 0, 0)  5.31 us
    ppermute x2, starting transfers between devices, swap_y(): return lax.ppermute(x, 'row', [(r, (r + 4) % 8) for r in range(8)])  4.76 us
  transfers between devices with their start and end apart: 25, of which 15 were waited for; matrix products, arithmetic and copies ran while one was open for 6% of the time, Pallas kernels for 21%

profile of v1, /device:TPU:8, one launch (start us, length us, event | category | flops | bytes accessed | tf_op | source)
XLA Modules:
  0.0 157.1 jit_solution(1389805936144594012)
XLA Ops:
  0.7 2.0 %fusion = f32[4,128,128]{2,0,1:T(4,128)S(1)} fusion(bf16[32,4]{0,1:T(4,128)(2,1)} %param.14, bf16[4,8,128,128]{3,2,1,0:T(8,128)(2,1)} %bitcast.93), kind=kOutput, calls=%fused_computation.3 | convolution fusion | flops 4194304 | bytes 1310976 | tf_op jit(solution)/shard_map/dot_general | solution.py:348
  3.3 2.3 %collective-permute-start.1 = (f32[128,128]{0,1:T(8,128)S(1)}, f32[128,128]{0,1:T(8,128)S(1)}, u32[]{:S(2)}, u32[]{:S(2)}) collective-permute-start(f32[128,128]{0,1:T(8,128)S(1)} %bitcast.91), channel_id=1, source_target_pairs={{0,2},{1,3},{2,0},{3,1},{4,6},{5,7},{6,4},{7,5},{8,10},{9,11},{10,... | collective-permute-start | bytes 196616 | tf_op jit(solution)/shard_map/ppermute | solution.py:310
  6.0 3.2 %collective-permute-done.1 = f32[128,128]{0,1:T(8,128)S(1)} collective-permute-done((f32[128,128]{0,1:T(8,128)S(1)}, f32[128,128]{0,1:T(8,128)S(1)}, u32[]{:S(2)}, u32[]{:S(2)}) %collective-permute-start.1) | collective-permute-done | bytes 65568 | tf_op jit(solution)/shard_map/ppermute | solution.py:310
  9.7 6.1 %collective-permute-start.4 = (f16[128,128]{1,0:T(8,128)(2,1)S(1)}, f16[128,128]{1,0:T(8,128)(2,1)S(1)}, u32[]{:S(2)}, u32[]{:S(2)}) collective-permute-start(f16[128,128]{1,0:T(8,128)(2,1)S(1)} %bitcast.78), channel_id=1, source_target_pairs={{0,20},{4,24},{8,28},{12,0},{16,4},{20,8},{24,12},{28,16},{1,21},{... | collective-permute-start | bytes 98312 | tf_op jit(solution)/shard_map/ppermute | solution.py:310
  15.9 2.0 %shard_map.119 = bf16[8,5,4,32,128]{4,3,2,1,0:T(8,128)(2,1)} custom-call(bf16[1,32,40,128]{3,2,1,0:T(8,128)(2,1)S(1)} %copy-done.4, bf16[1,32,40,128]{3,2,1,0:T(8,128)(2,1)S(1)} %copy-done.5, bf16[1,32,40,128]{3,2,1,0:T(8,128)(2,1)S(1)} %copy-done.6, bf16[1,32,40,128]{3,2,1,0:T(8,128)(2,1)S(1)} %copy-done, bf16[1,32,40,128]{3,2,1,0:T(8,128)(2,1)S(1)} %copy-done.1), custom_call_target="tpu_custom_call" | custom-call | tf_op jit(solution)/shard_map/pallas_call | solution.py:287
  17.8 4.9 %collective-permute-done.3 = f16[128,128]{1,0:T(8,128)(2,1)S(1)} collective-permute-done((f16[128,128]{1,0:T(8,128)(2,1)S(1)}, f16[128,128]{1,0:T(8,128)(2,1)S(1)}, u32[]{:S(2)}, u32[]{:S(2)}) %collective-permute-start.3) | collective-permute-done | bytes 32800 | tf_op jit(solution)/shard_map/ppermute | solution.py:310
  23.9 2.3 %collective-permute-start.6 = (f16[2,128,128]{2,1,0:T(8,128)(2,1)S(1)}, f16[2,128,128]{2,1,0:T(8,128)(2,1)S(1)}, u32[]{:S(2)}, u32[]{:S(2)}) collective-permute-start(f16[2,128,128]{2,1,0:T(8,128)(2,1)S(1)} %pad_maximum_fusion.3), channel_id=1, source_target_pairs={{0,28},{4,0},{8,4},{12,8},{16,12},{20,16},{24,20},{28,24},{1,29},{... | collective-permute-start | bytes 196616 | tf_op jit(solution)/shard_map/ppermute | solution.py:310
  26.2 2.5 %collective-permute-done.5 = f16[3,128,128]{2,1,0:T(8,128)(2,1)S(1)} collective-permute-done((f16[3,128,128]{2,1,0:T(8,128)(2,1)S(1)}, f16[3,128,128]{2,1,0:T(8,128)(2,1)S(1)}, u32[]{:S(2)}, u32[]{:S(2)}) %collective-permute-start.5) | collective-permute-done | bytes 98336 | tf_op jit(solution)/shard_map/ppermute | solution.py:310
  28.9 4.2 %all-to-all-start = ((bf16[8,5,4,32,128]{4,3,2,1,0:T(8,128)(2,1)}), bf16[8,5,4,32,128]{4,3,2,1,0:T(8,128)(2,1)S(1)}, u32[]{:S(2)}, u32[]{:S(2)}) async-start(bf16[8,5,4,32,128]{4,3,2,1,0:T(8,128)(2,1)} %shard_map.119), calls=%async_computation | async-start | bytes 2621440 | tf_op jit(solution)/shard_map/all_to_all | solution.py:362
  33.1 2.4 %collective-permute-start.7 = (f16[8,128,128]{2,1,0:T(8,128)(2,1)S(1)}, f16[8,128,128]{2,1,0:T(8,128)(2,1)S(1)}, u32[]{:S(2)}, u32[]{:S(2)}) collective-permute-start(f16[8,128,128]{2,1,0:T(8,128)(2,1)S(1)} %slice_dynamic-update-slice_fusion), channel_id=1, source_target_pairs={{0,128},{32,160},{64,192},{96,224},{128,0},{160,32},{192,64},{224,... | collective-permute-start | bytes 786440 | tf_op jit(solution)/shard_map/ppermute | solution.py:318
  35.5 5.6 %collective-permute-done.7 = f16[8,128,128]{2,1,0:T(8,128)(2,1)S(1)} collective-permute-done((f16[8,128,128]{2,1,0:T(8,128)(2,1)S(1)}, f16[8,128,128]{2,1,0:T(8,128)(2,1)S(1)}, u32[]{:S(2)}, u32[]{:S(2)}) %collective-permute-start.7) | collective-permute-done | bytes 262176 | tf_op jit(solution)/shard_map/ppermute | solution.py:318
  42.1 3.0 %collective-permute-start.10 = (f16[2,8,128,128]{3,2,1,0:T(8,128)(2,1)}, f16[2,8,128,128]{3,2,1,0:T(8,128)(2,1)}, u32[]{:S(2)}, u32[]{:S(2)}) collective-permute-start(f16[2,8,128,128]{3,2,1,0:T(8,128)(2,1)} %get-tuple-element.79), channel_id=1, source_target_pairs={{0,64},{32,96},{64,0},{96,32},{128,192},{160,224},{192,128},{224,1... | collective-permute-start | bytes 1572872 | tf_op jit(solution)/shard_map/ppermute | solution.py:314
  45.7 2.6 %collective-permute-start.9 = (f16[2,8,128,128]{3,2,1,0:T(8,128)(2,1)}, f16[2,8,128,128]{3,2,1,0:T(8,128)(2,1)}, u32[]{:S(2)}, u32[]{:S(2)}) collective-permute-start(f16[2,8,128,128]{3,2,1,0:T(8,128)(2,1)} %get-tuple-element.79), channel_id=1, source_target_pairs={{0,96},{32,0},{64,32},{96,64},{128,224},{160,128},{192,160},{224,1... | collective-permute-start | bytes 1572872 | tf_op jit(solution)/shard_map/ppermute | solution.py:314
  49.7 8.5 %collective-permute-done.10 = f16[2,8,128,128]{3,2,1,0:T(8,128)(2,1)} collective-permute-done((f16[2,8,128,128]{3,2,1,0:T(8,128)(2,1)}, f16[2,8,128,128]{3,2,1,0:T(8,128)(2,1)}, u32[]{:S(2)}, u32[]{:S(2)}) %collective-permute-start.10) | collective-permute-done | bytes 524320 | tf_op jit(solution)/shard_map/ppermute | solution.py:314
  58.2 2.1 %convert_element_type.67.refs_2_ = f32[2,8,128,128]{3,2,1,0:T(8,128)} convert(f16[2,8,128,128]{3,2,1,0:T(8,128)(2,1)} %collective-permute-done.10) | non-fusion elementwise | flops 262144 | bytes 1572864 | tf_op jit(solution)/shard_map/convert_element_type | solution.py:366
  60.3 3.5 %all-to-all-done.refs_1_ = bf16[8,5,4,32,128]{4,3,2,1,0:T(8,128)(2,1)S(1)} async-done(((bf16[8,5,4,32,128]{4,3,2,1,0:T(8,128)(2,1)}), bf16[8,5,4,32,128]{4,3,2,1,0:T(8,128)(2,1)S(1)}, u32[]{:S(2)}, u32[]{:S(2)}) %all-to-all-start) | async-done | bytes 1310752 | tf_op jit(solution)/shard_map/all_to_all | solution.py:362
  65.1 8.8 %shard_map.120 = (bf16[8,5,2,32,128]{4,3,2,1,0:T(8,128)(2,1)S(1)}, bf16[2,8,128,128]{3,2,1,0:T(8,128)(2,1)S(1)}, bf16[5,1024,128]{2,1,0:T(8,128)(2,1)S(1)}, bf16...) custom-call(s32[10]{0:T(128)S(1)} %pad_add_fusion.refs_0_, bf16[8,5,4,32,128]{4,3,2,1,0:T(8,128)(2,1)S(1)} %all-to-all-done.refs_1_, ...), custom_call_target="tpu_custom_call" | custom-call | flops 2000000000 | bytes 8000000 | tf_op jit(solution)/shard_map/pallas_call | solution.py:253
  75.1 3.1 %collective-permute-start.11 = (bf16[2,8,128,128]{3,2,1,0:T(8,128)(2,1)S(1)}, bf16[2,8,128,128]{3,2,1,0:T(8,128)(2,1)S(1)}, u32[]{:S(2)}, u32[]{:S(2)}) collective-permute-start(bf16[2,8,128,128]{3,2,1,0:T(8,128)(2,1)S(1)} %get-tuple-element.50), channel_id=1, source_target_pairs={{0,64},{32,96},{64,0},{96,32},{128,192},{160,224},{192,128},{224,1... | collective-permute-start | bytes 1572872 | tf_op jit(solution)/shard_map/ppermute | solution.py:314
  78.2 12.2 %shard_map.121 = (bf16[8,5,2,32,128]{4,3,2,1,0:T(8,128)(2,1)S(1)}, bf16[2,8,128,128]{3,2,1,0:T(8,128)(2,1)S(1)}, bf16[2,8,128,128]{3,2,1,0:T(8,128)(2,1)S(1)}, b...) custom-call(s32[10]{0:T(128)S(1)} %pad_add_fusion.refs_0_, ...), custom_call_target="tpu_custom_call" | custom-call | flops 4000000000 | bytes 8000000 | tf_op jit(solution)/shard_map/pallas_call | solution.py:253
  91.1 2.7 %collective-permute-start.12 = (bf16[2,8,128,128]{3,2,1,0:T(8,128)(2,1)S(1)}, bf16[2,8,128,128]{3,2,1,0:T(8,128)(2,1)S(1)}, u32[]{:S(2)}, u32[]{:S(2)}) collective-permute-start(bf16[2,8,128,128]{3,2,1,0:T(8,128)(2,1)S(1)} %get-tuple-element.53), channel_id=1, source_target_pairs={{0,96},{32,0},{64,32},{96,64},{128,224},{160,128},{192,160},{224,1... | collective-permute-start | bytes 1572872 | tf_op jit(solution)/shard_map/ppermute | solution.py:314
  93.7 9.4 %shard_map.122 = (bf16[8,5,2,32,128]{4,3,2,1,0:T(8,128)(2,1)S(1)}, bf16[8,5,2,32,128]{4,3,2,1,0:T(8,128)(2,1)}, f32[2,8,128,128]{3,2,1,0:T(8,128)S(1)}) custom-call(s32[10]{0:T(128)S(1)} %pad_add_fusion.refs_0_, bf16[8,5,4,32,128]{4,3,2,1,0:T(8,128)(2,1)S(1)} %all-to-all-done.refs_1_, f32[2,8,128,128]{3,2,1,0:T(8,128)S(1)} %get-tuple-element.80.refs_2_, ...), custom_call_target="tpu_custom_call" | custom-call | flops 2000000000 | bytes 8000000 | tf_op jit(solution)/shard_map/pallas_call | solution.py:253
  104.0 2.4 %collective-permute-start.14 = (bf16[8,128,128]{2,1,0:T(8,128)(2,1)S(1)}, bf16[8,128,128]{2,1,0:T(8,128)(2,1)S(1)}, u32[]{:S(2)}, u32[]{:S(2)}) collective-permute-start(bf16[8,128,128]{2,1,0:T(8,128)(2,1)S(1)} %fusion.4), channel_id=1, source_target_pairs={{0,128},{32,160},{64,192},{96,224},{128,0},{160,32},{192,64},{224,... | collective-permute-start | bytes 786440 | tf_op jit(solution)/shard_map/ppermute | solution.py:318
  106.4 3.5 %all-to-all-start.1 = ((bf16[8,5,2,32,128]{4,3,2,1,0:T(8,128)(2,1)}), bf16[8,5,2,32,128]{4,3,2,1,0:T(8,128)(2,1)S(1)}, u32[]{:S(2)}, u32[]{:S(2)}) async-start(bf16[8,5,2,32,128]{4,3,2,1,0:T(8,128)(2,1)} %copy-done.3), calls=%async_computation.1 | async-start | bytes 1310720 | tf_op jit(solution)/shard_map/all_to_all | solution.py:373
  109.9 2.0 %collective-permute-done.14 = bf16[8,128,128]{2,1,0:T(8,128)(2,1)S(1)} collective-permute-done((bf16[8,128,128]{2,1,0:T(8,128)(2,1)S(1)}, bf16[8,128,128]{2,1,0:T(8,128)(2,1)S(1)}, u32[]{:S(2)}, u32[]{:S(2)}) %collective-permute-start.14) | collective-permute-done | bytes 262176 | tf_op jit(solution)/shard_map/ppermute | solution.py:318
  114.3 8.8 %collective-permute-done.16 = bf16[2,128,128]{2,1,0:T(8,128)(2,1)S(1)} collective-permute-done((bf16[2,128,128]{2,1,0:T(8,128)(2,1)S(1)}, bf16[2,128,128]{2,1,0:T(8,128)(2,1)S(1)}, u32[]{:S(2)}, u32[]{:S(2)}) %collective-permute-start.16) | collective-permute-done | bytes 65568 | tf_op jit(solution)/shard_map/ppermute | solution.py:310
  124.4 3.9 %collective-permute-start.17 = (bf16[128,128]{1,0:T(8,128)(2,1)S(1)}, bf16[128,128]{1,0:T(8,128)(2,1)S(1)}, u32[]{:S(2)}, u32[]{:S(2)}) collective-permute-start(bf16[128,128]{1,0:T(8,128)(2,1)S(1)} %get-tuple-element.78), channel_id=1, source_target_pairs={{0,20},{4,24},{8,28},{12,0},{16,4},{20,8},{24,12},{28,16},{1,21},{... | collective-permute-start | bytes 98312 | tf_op jit(solution)/shard_map/ppermute | solution.py:310
  131.5 3.7 %collective-permute-done.18 = bf16[128,128]{1,0:T(8,128)(2,1)S(1)} collective-permute-done((bf16[128,128]{1,0:T(8,128)(2,1)S(1)}, bf16[128,128]{1,0:T(8,128)(2,1)S(1)}, u32[]{:S(2)}, u32[]{:S(2)}) %collective-permute-start.18) | collective-permute-done | bytes 32800 | tf_op jit(solution)/shard_map/ppermute | solution.py:310
  135.2 5.3 %all-to-all-start.2 = ((bf16[8,5,2,32,128]{4,3,2,1,0:T(8,128)(2,1)}), bf16[8,5,2,32,128]{4,3,2,1,0:T(8,128)(2,1)S(1)}, u32[]{:S(2)}, u32[]{:S(2)}) async-start(bf16[8,5,2,32,128]{4,3,2,1,0:T(8,128)(2,1)} %get-tuple-element.56), calls=%async_computation.2 | async-start | bytes 1310720 | tf_op jit(solution)/shard_map/all_to_all | solution.py:377
  141.3 1.9 %collective-permute-start.20 = (f32[128,128]{0,1:T(8,128)S(1)}, f32[128,128]{0,1:T(8,128)S(1)}, u32[]{:S(2)}, u32[]{:S(2)}) collective-permute-start(f32[128,128]{0,1:T(8,128)S(1)} %fusion.14), channel_id=1, source_target_pairs={{0,2},{1,3},{2,0},{3,1},{4,6},{5,7},{6,4},{7,5},{8,10},{9,11},{10,... | collective-permute-start | bytes 196616 | tf_op jit(solution)/shard_map/ppermute | solution.py:310
  143.5 3.3 %collective-permute-done.20 = f32[128,128]{0,1:T(8,128)S(1)} collective-permute-done((f32[128,128]{0,1:T(8,128)S(1)}, f32[128,128]{0,1:T(8,128)S(1)}, u32[]{:S(2)}, u32[]{:S(2)}) %collective-permute-start.20) | collective-permute-done | bytes 65568 | tf_op jit(solution)/shard_map/ppermute | solution.py:310
  147.3 2.1 %convolution_convert_fusion = bf16[32,128,128]{2,0,1:T(8,128)(2,1)S(1)} fusion(f32[1,16384]{1,0:T(1,128)S(1)} %bitcast.85, f32[1,16384]{1,0:T(1,128)S(1)} %bitcast.86, f32[1,16384]{1,0:T(1,128)S(1)} %bitcast.87, f32[1,16384]{1,0:T(1,128)S(1)} %bitcast.84, f32[4,32]{1,0:T(4,128)S(1)} %gather_fusion, pred[4]{0:T(512)(128)(4,1)S(1)} %compare_and_fusion), kind=kOutput, calls=%fused_computation.1 | convolution fusion | flops 25886848 | bytes 1311236 | tf_op jit(solution)/shard_map/dot_general | solution.py:384
  150.7 4.5 %all-to-all-done.2.z_ref = bf16[8,5,2,32,128]{4,3,2,1,0:T(8,128)(2,1)S(1)} async-done(((bf16[8,5,2,32,128]{4,3,2,1,0:T(8,128)(2,1)}), bf16[8,5,2,32,128]{4,3,2,1,0:T(8,128)(2,1)S(1)}, u32[]{:S(2)}, u32[]{:S(2)}) %all-to-all-start.2) | async-done | bytes 655392 | tf_op jit(solution)/shard_map/all_to_all | solution.py:377
  (87 shorter events, 21.2 us)
Async XLA Ops:
  0.7 15.1 %copy-start = (bf16[1,32,40,128]{3,2,1,0:T(8,128)(2,1)S(1)}, bf16[1,32,40,128]{3,2,1,0:T(8,128)(2,1)}, u32[]{:S(2)}) copy-start(bf16[1,32,40,128]{3,2,1,0:T(8,128)(2,1)} %g_ref.3) | copy-start | bytes 983044
  0.7 15.1 %copy-start.1 = (bf16[1,32,40,128]{3,2,1,0:T(8,128)(2,1)S(1)}, bf16[1,32,40,128]{3,2,1,0:T(8,128)(2,1)}, u32[]{:S(2)}) copy-start(bf16[1,32,40,128]{3,2,1,0:T(8,128)(2,1)} %c_ref.3) | copy-start | bytes 983044
  0.7 15.1 %copy-start.4 = (bf16[1,32,40,128]{3,2,1,0:T(8,128)(2,1)S(1)}, bf16[1,32,40,128]{3,2,1,0:T(8,128)(2,1)}, u32[]{:S(2)}) copy-start(bf16[1,32,40,128]{3,2,1,0:T(8,128)(2,1)} %q_ref.1) | copy-start | bytes 983044
  0.7 15.1 %copy-start.5 = (bf16[1,32,40,128]{3,2,1,0:T(8,128)(2,1)S(1)}, bf16[1,32,40,128]{3,2,1,0:T(8,128)(2,1)}, u32[]{:S(2)}) copy-start(bf16[1,32,40,128]{3,2,1,0:T(8,128)(2,1)} %k_ref.1) | copy-start | bytes 983044
  0.7 15.1 %copy-start.6 = (bf16[1,32,40,128]{3,2,1,0:T(8,128)(2,1)S(1)}, bf16[1,32,40,128]{3,2,1,0:T(8,128)(2,1)}, u32[]{:S(2)}) copy-start(bf16[1,32,40,128]{3,2,1,0:T(8,128)(2,1)} %v_ref.1) | copy-start | bytes 983044
  3.1 2.9 %collective-permute-start.2 = (f32[128,128]{0,1:T(8,128)S(1)}, f32[128,128]{0,1:T(8,128)S(1)}, u32[]{:S(2)}, u32[]{:S(2)}) collective-permute-start(f32[128,128]{0,1:T(8,128)S(1)} %bitcast.90), channel_id=1, source_target_pairs={{0,3},{1,0},{2,1},{3,2},{4,7},{5,4},{6,5},{7,6},{8,11},{9,8},{10,9... | collective-permute-start | bytes 196616 | tf_op jit(solution)/shard_map/ppermute | solution.py:310
  3.3 6.0 %collective-permute-start.1 = (f32[128,128]{0,1:T(8,128)S(1)}, f32[128,128]{0,1:T(8,128)S(1)}, u32[]{:S(2)}, u32[]{:S(2)}) collective-permute-start(f32[128,128]{0,1:T(8,128)S(1)} %bitcast.91), channel_id=1, source_target_pairs={{0,2},{1,3},{2,0},{3,1},{4,6},{5,7},{6,4},{7,5},{8,10},{9,11},{10,... | collective-permute-start | bytes 196616 | tf_op jit(solution)/shard_map/ppermute | solution.py:310
  5.6 4.1 %collective-permute-start = (f32[128,128]{0,1:T(8,128)S(1)}, f32[128,128]{0,1:T(8,128)S(1)}, u32[]{:S(2)}, u32[]{:S(2)}) collective-permute-start(f32[128,128]{0,1:T(8,128)S(1)} %bitcast.92), channel_id=1, source_target_pairs={{0,1},{1,2},{2,3},{3,0},{4,5},{5,6},{6,7},{7,4},{8,9},{9,10},{10,1... | collective-permute-start | bytes 196616 | tf_op jit(solution)/shard_map/ppermute | solution.py:310
  9.7 8.1 %collective-permute-start.4 = (f16[128,128]{1,0:T(8,128)(2,1)S(1)}, f16[128,128]{1,0:T(8,128)(2,1)S(1)}, u32[]{:S(2)}, u32[]{:S(2)}) collective-permute-start(f16[128,128]{1,0:T(8,128)(2,1)S(1)} %bitcast.78), channel_id=1, source_target_pairs={{0,20},{4,24},{8,28},{12,0},{16,4},{20,8},{24,12},{28,16},{1,21},{... | collective-permute-start | bytes 98312 | tf_op jit(solution)/shard_map/ppermute | solution.py:310
  15.8 7.0 %collective-permute-start.3 = (f16[128,128]{1,0:T(8,128)(2,1)S(1)}, f16[128,128]{1,0:T(8,128)(2,1)S(1)}, u32[]{:S(2)}, u32[]{:S(2)}) collective-permute-start(f16[128,128]{1,0:T(8,128)(2,1)S(1)} %bitcast.79), channel_id=1, source_target_pairs={{0,12},{4,16},{8,20},{12,24},{16,28},{20,0},{24,4},{28,8},{1,13},{... | collective-permute-start | bytes 98312 | tf_op jit(solution)/shard_map/ppermute | solution.py:310
  22.8 5.9 %collective-permute-start.5 = (f16[3,128,128]{2,1,0:T(8,128)(2,1)S(1)}, f16[3,128,128]{2,1,0:T(8,128)(2,1)S(1)}, u32[]{:S(2)}, u32[]{:S(2)}) collective-permute-start(f16[3,128,128]{2,1,0:T(8,128)(2,1)S(1)} %pad_maximum_fusion.1), channel_id=1, source_target_pairs={{0,4},{4,8},{8,12},{12,16},{16,20},{20,24},{24,28},{28,0},{1,5},{5... | collective-permute-start | bytes 294920 | tf_op jit(solution)/shard_map/ppermute | solution.py:310
  23.9 4.8 %collective-permute-start.6 = (f16[2,128,128]{2,1,0:T(8,128)(2,1)S(1)}, f16[2,128,128]{2,1,0:T(8,128)(2,1)S(1)}, u32[]{:S(2)}, u32[]{:S(2)}) collective-permute-start(f16[2,128,128]{2,1,0:T(8,128)(2,1)S(1)} %pad_maximum_fusion.3), channel_id=1, source_target_pairs={{0,28},{4,0},{8,4},{12,8},{16,12},{20,16},{24,20},{28,24},{1,29},{... | collective-permute-start | bytes 196616 | tf_op jit(solution)/shard_map/ppermute | solution.py:310
  28.9 34.9 %all-to-all-start = ((bf16[8,5,4,32,128]{4,3,2,1,0:T(8,128)(2,1)}), bf16[8,5,4,32,128]{4,3,2,1,0:T(8,128)(2,1)S(1)}, u32[]{:S(2)}, u32[]{:S(2)}) async-start(bf16[8,5,4,32,128]{4,3,2,1,0:T(8,128)(2,1)} %shard_map.119), calls=%async_computation | async-start | bytes 2621440 | tf_op jit(solution)/shard_map/all_to_all | solution.py:362
  33.1 15.2 %copy-start.8 = (s32[8]{0:T(128)S(1)}, s32[8]{0:T(128)}, u32[]{:S(2)}) copy-start(s32[8]{0:T(128)} %param.15) | copy-start | bytes 100
  33.1 8.0 %collective-permute-start.7 = (f16[8,128,128]{2,1,0:T(8,128)(2,1)S(1)}, f16[8,128,128]{2,1,0:T(8,128)(2,1)S(1)}, u32[]{:S(2)}, u32[]{:S(2)}) collective-permute-start(f16[8,128,128]{2,1,0:T(8,128)(2,1)S(1)} %slice_dynamic-update-slice_fusion), channel_id=1, source_target_pairs={{0,128},{32,160},{64,192},{96,224},{128,0},{160,32},{192,64},{224,... | collective-permute-start | bytes 786440 | tf_op jit(solution)/shard_map/ppermute | solution.py:318
  42.1 16.1 %collective-permute-start.10 = (f16[2,8,128,128]{3,2,1,0:T(8,128)(2,1)}, f16[2,8,128,128]{3,2,1,0:T(8,128)(2,1)}, u32[]{:S(2)}, u32[]{:S(2)}) collective-permute-start(f16[2,8,128,128]{3,2,1,0:T(8,128)(2,1)} %get-tuple-element.79), channel_id=1, source_target_pairs={{0,64},{32,96},{64,0},{96,32},{128,192},{160,224},{192,128},{224,1... | collective-permute-start | bytes 1572872 | tf_op jit(solution)/shard_map/ppermute | solution.py:314
  45.1 28.7 %collective-permute-start.8 = (f16[2,8,128,128]{3,2,1,0:T(8,128)(2,1)}, f16[2,8,128,128]{3,2,1,0:T(8,128)(2,1)S(1)}, u32[]{:S(2)}, u32[]{:S(2)}) collective-permute-start(f16[2,8,128,128]{3,2,1,0:T(8,128)(2,1)} %get-tuple-element.79), channel_id=1, source_target_pairs={{0,32},{32,64},{64,96},{96,0},{128,160},{160,192},{192,224},{224,1... | collective-permute-start | bytes 1572872 | tf_op jit(solution)/shard_map/ppermute | solution.py:314
  45.7 28.2 %collective-permute-start.9 = (f16[2,8,128,128]{3,2,1,0:T(8,128)(2,1)}, f16[2,8,128,128]{3,2,1,0:T(8,128)(2,1)}, u32[]{:S(2)}, u32[]{:S(2)}) collective-permute-start(f16[2,8,128,128]{3,2,1,0:T(8,128)(2,1)} %get-tuple-element.79), channel_id=1, source_target_pairs={{0,96},{32,0},{64,32},{96,64},{128,224},{160,128},{192,160},{224,1... | collective-permute-start | bytes 1572872 | tf_op jit(solution)/shard_map/ppermute | solution.py:314
  75.1 18.6 %collective-permute-start.11 = (bf16[2,8,128,128]{3,2,1,0:T(8,128)(2,1)S(1)}, bf16[2,8,128,128]{3,2,1,0:T(8,128)(2,1)S(1)}, u32[]{:S(2)}, u32[]{:S(2)}) collective-permute-start(bf16[2,8,128,128]{3,2,1,0:T(8,128)(2,1)S(1)} %get-tuple-element.50), channel_id=1, source_target_pairs={{0,64},{32,96},{64,0},{96,32},{128,192},{160,224},{192,128},{224,1... | collective-permute-start | bytes 1572872 | tf_op jit(solution)/shard_map/ppermute | solution.py:314
  90.4 12.7 %collective-permute-start.13 = (bf16[2,8,128,128]{3,2,1,0:T(8,128)(2,1)S(1)}, bf16[2,8,128,128]{3,2,1,0:T(8,128)(2,1)S(1)}, u32[]{:S(2)}, u32[]{:S(2)}) collective-permute-start(bf16[2,8,128,128]{3,2,1,0:T(8,128)(2,1)S(1)} %get-tuple-element.54), channel_id=1, source_target_pairs={{0,32},{32,64},{64,96},{96,0},{128,160},{160,192},{192,224},{224,1... | collective-permute-start | bytes 1572872 | tf_op jit(solution)/shard_map/ppermute | solution.py:314
  91.1 12.1 %collective-permute-start.12 = (bf16[2,8,128,128]{3,2,1,0:T(8,128)(2,1)S(1)}, bf16[2,8,128,128]{3,2,1,0:T(8,128)(2,1)S(1)}, u32[]{:S(2)}, u32[]{:S(2)}) collective-permute-start(bf16[2,8,128,128]{3,2,1,0:T(8,128)(2,1)S(1)} %get-tuple-element.53), channel_id=1, source_target_pairs={{0,96},{32,0},{64,32},{96,64},{128,224},{160,128},{192,160},{224,1... | collective-permute-start | bytes 1572872 | tf_op jit(solution)/shard_map/ppermute | solution.py:314
  104.0 8.0 %collective-permute-start.14 = (bf16[8,128,128]{2,1,0:T(8,128)(2,1)S(1)}, bf16[8,128,128]{2,1,0:T(8,128)(2,1)S(1)}, u32[]{:S(2)}, u32[]{:S(2)}) collective-permute-start(bf16[8,128,128]{2,1,0:T(8,128)(2,1)S(1)} %fusion.4), channel_id=1, source_target_pairs={{0,128},{32,160},{64,192},{96,224},{128,0},{160,32},{192,64},{224,... | collective-permute-start | bytes 786440 | tf_op jit(solution)/shard_map/ppermute | solution.py:318
  106.4 28.8 %all-to-all-start.1 = ((bf16[8,5,2,32,128]{4,3,2,1,0:T(8,128)(2,1)}), bf16[8,5,2,32,128]{4,3,2,1,0:T(8,128)(2,1)S(1)}, u32[]{:S(2)}, u32[]{:S(2)}) async-start(bf16[8,5,2,32,128]{4,3,2,1,0:T(8,128)(2,1)} %copy-done.3), calls=%async_computation.1 | async-start | bytes 1310720 | tf_op jit(solution)/shard_map/all_to_all | solution.py:373
  112.1 28.4 %copy-start.7 = (bf16[32,4]{0,1:T(4,128)(2,1)S(1)}, bf16[32,4]{0,1:T(4,128)(2,1)}, u32[]{:S(2)}) copy-start(bf16[32,4]{0,1:T(4,128)(2,1)} %param.14) | copy-start | bytes 772
  112.1 12.2 %collective-permute-start.15 = (bf16[3,128,128]{2,1,0:T(8,128)(2,1)S(1)}, bf16[3,128,128]{2,1,0:T(8,128)(2,1)S(1)}, u32[]{:S(2)}, u32[]{:S(2)}) collective-permute-start(bf16[3,128,128]{2,1,0:T(8,128)(2,1)S(1)} %pad_maximum_fusion.2), channel_id=1, source_target_pairs={{0,28},{4,0},{8,4},{12,8},{16,12},{20,16},{24,20},{28,24},{1,29},{... | collective-permute-start | bytes 294920 | tf_op jit(solution)/shard_map/ppermute | solution.py:310
  113.3 9.8 %collective-permute-start.16 = (bf16[2,128,128]{2,1,0:T(8,128)(2,1)S(1)}, bf16[2,128,128]{2,1,0:T(8,128)(2,1)S(1)}, u32[]{:S(2)}, u32[]{:S(2)}) collective-permute-start(bf16[2,128,128]{2,1,0:T(8,128)(2,1)S(1)} %pad_maximum_fusion.4), channel_id=1, source_target_pairs={{0,4},{4,8},{8,12},{12,16},{16,20},{20,24},{24,28},{28,0},{1,5},{5... | collective-permute-start | bytes 196616 | tf_op jit(solution)/shard_map/ppermute | solution.py:310
  124.4 7.2 %collective-permute-start.17 = (bf16[128,128]{1,0:T(8,128)(2,1)S(1)}, bf16[128,128]{1,0:T(8,128)(2,1)S(1)}, u32[]{:S(2)}, u32[]{:S(2)}) collective-permute-start(bf16[128,128]{1,0:T(8,128)(2,1)S(1)} %get-tuple-element.78), channel_id=1, source_target_pairs={{0,20},{4,24},{8,28},{12,0},{16,4},{20,8},{24,12},{28,16},{1,21},{... | collective-permute-start | bytes 98312 | tf_op jit(solution)/shard_map/ppermute | solution.py:310
  128.3 6.9 %collective-permute-start.18 = (bf16[128,128]{1,0:T(8,128)(2,1)S(1)}, bf16[128,128]{1,0:T(8,128)(2,1)S(1)}, u32[]{:S(2)}, u32[]{:S(2)}) collective-permute-start(bf16[128,128]{1,0:T(8,128)(2,1)S(1)} %get-tuple-element.77), channel_id=1, source_target_pairs={{0,12},{4,16},{8,20},{12,24},{16,28},{20,0},{24,4},{28,8},{1,13},{... | collective-permute-start | bytes 98312 | tf_op jit(solution)/shard_map/ppermute | solution.py:310
  135.2 20.0 %all-to-all-start.2 = ((bf16[8,5,2,32,128]{4,3,2,1,0:T(8,128)(2,1)}), bf16[8,5,2,32,128]{4,3,2,1,0:T(8,128)(2,1)S(1)}, u32[]{:S(2)}, u32[]{:S(2)}) async-start(bf16[8,5,2,32,128]{4,3,2,1,0:T(8,128)(2,1)} %get-tuple-element.56), calls=%async_computation.2 | async-start | bytes 1310720 | tf_op jit(solution)/shard_map/all_to_all | solution.py:377
  141.2 2.2 %collective-permute-start.21 = (f32[128,128]{0,1:T(8,128)S(1)}, f32[128,128]{0,1:T(8,128)S(1)}, u32[]{:S(2)}, u32[]{:S(2)}) collective-permute-start(f32[128,128]{0,1:T(8,128)S(1)} %fusion.14), channel_id=1, source_target_pairs={{0,3},{1,0},{2,1},{3,2},{4,7},{5,4},{6,5},{7,6},{8,11},{9,8},{10,9... | collective-permute-start | bytes 196616 | tf_op jit(solution)/shard_map/ppermute | solution.py:310
  141.3 5.5 %collective-permute-start.20 = (f32[128,128]{0,1:T(8,128)S(1)}, f32[128,128]{0,1:T(8,128)S(1)}, u32[]{:S(2)}, u32[]{:S(2)}) collective-permute-start(f32[128,128]{0,1:T(8,128)S(1)} %fusion.14), channel_id=1, source_target_pairs={{0,2},{1,3},{2,0},{3,1},{4,6},{5,7},{6,4},{7,5},{8,10},{9,11},{10,... | collective-permute-start | bytes 196616 | tf_op jit(solution)/shard_map/ppermute | solution.py:310
  143.1 4.1 %collective-permute-start.19 = (f32[128,128]{0,1:T(8,128)S(1)}, f32[128,128]{0,1:T(8,128)S(1)}, u32[]{:S(2)}, u32[]{:S(2)}) collective-permute-start(f32[128,128]{0,1:T(8,128)S(1)} %fusion.14), channel_id=1, source_target_pairs={{0,1},{1,2},{2,3},{3,0},{4,5},{5,6},{6,7},{7,4},{8,9},{9,10},{10,1... | collective-permute-start | bytes 196616 | tf_op jit(solution)/shard_map/ppermute | solution.py:310
  (2 other events, 2.1 us)

commit v2 on v1

--- a/solution.py
+++ b/solution.py
@@ -32,19 +32,28 @@
                 x_ref[dest, r, a] = part
 
 
-def merge_kernel(y_ref, z_ref, g_ref, c_ref, dq_ref, dk_ref, dv_ref, dg_ref, buf):
-    cols, per = y_ref.shape[:2]
-    rows = dq_ref.shape[2]
+def merge_kernel(x_ref, first_ref, second_ref, buf):
+    cols, per = x_ref.shape[:2]
+    rows = first_ref.shape[2]
     for src in range(cols):
         for r in range(per):
-            for a in range(4):
-                part = z_ref[src, r, a - 1] if a in (1, 2) else y_ref[src, r, a // 3]
-                buf[a, pl.ds(r * cols + src, DIM, rows)] = part.astype(F32)
-    for a, out in enumerate((dq_ref, dk_ref, dv_ref)):
+            for a in range(2):
+                buf[a, pl.ds(r * cols + src, DIM, rows)] = x_ref[src, r, a].astype(F32)
+    for a, out in enumerate((first_ref, second_ref)):
         out[0] = buf[a].reshape(DIM, rows, BLK).astype(BF)
+
+
+def merge_gate_kernel(x_ref, g_ref, c_ref, first_ref, gate_ref, buf):
+    cols, per = x_ref.shape[:2]
+    rows = first_ref.shape[2]
+    for src in range(cols):
+        for r in range(per):
+            for a in range(2):
+                buf[a, pl.ds(r * cols + src, DIM, rows)] = x_ref[src, r, a].astype(F32)
+    first_ref[0] = buf[0].reshape(DIM, rows, BLK).astype(BF)
     gate = jax.nn.sigmoid(g_ref[0].astype(F32))
-    attended = buf[3].reshape(DIM, rows, BLK)
-    dg_ref[0] = (c_ref[0].astype(F32) * attended * gate * (1.0 - gate)).astype(BF)
+    attended = buf[1].reshape(DIM, rows, BLK)
+    gate_ref[0] = (c_ref[0].astype(F32) * attended * gate * (1.0 - gate)).astype(BF)
 
 
 def attend_kernel(ts, first, last, extra, *refs):
@@ -267,7 +276,7 @@
             pltpu.VMEM((len(ts),) + tile_shape, F32),
         ],
         compiler_params=pltpu.CompilerParams(
-            vmem_limit_bytes=(18 if len(ts) > 1 else 11) * 1024 * 1024
+            vmem_limit_bytes=(14 if len(ts) > 1 else 8) * 1024 * 1024
         ),
         cost_estimate=pl.CostEstimate(
             flops=len(ts) * 2_000_000_000, bytes_accessed=8_000_000, transcendentals=0
@@ -290,20 +299,20 @@
         out_specs=VMEM_SPEC,
         out_shape=jax.ShapeDtypeStruct((cols, rows // cols, 4, DIM, BLK), BF),
         scratch_shapes=[pltpu.VMEM((4, DIM * rows, BLK), F32)],
-        compiler_params=pltpu.CompilerParams(vmem_limit_bytes=8 * 1024 * 1024),
+        compiler_params=pltpu.CompilerParams(vmem_limit_bytes=5 * 1024 * 1024),
     )(q, k, v, g, c)
 
 
-def merge(y, z, g, c):
-    rows = g.shape[2]
+def merge(x, shape, *gates):
+    rows = shape[2]
     return pl.pallas_call(
-        merge_kernel,
-        in_specs=[VMEM_SPEC] * 4,
-        out_specs=[VMEM_SPEC] * 4,
-        out_shape=[jax.ShapeDtypeStruct(g.shape, BF)] * 4,
-        scratch_shapes=[pltpu.VMEM((4, DIM * rows, BLK), F32)],
-        compiler_params=pltpu.CompilerParams(vmem_limit_bytes=8 * 1024 * 1024),
-    )(y, z, g, c)
+        merge_gate_kernel if gates else merge_kernel,
+        in_specs=[VMEM_SPEC] * (1 + len(gates)),
+        out_specs=[VMEM_SPEC] * 2,
+        out_shape=[jax.ShapeDtypeStruct(shape, BF)] * 2,
+        scratch_shapes=[pltpu.VMEM((2, DIM * rows, BLK), F32)],
+        compiler_params=pltpu.CompilerParams(vmem_limit_bytes=5 * 1024 * 1024),
+    )(x, *gates)
 
 
 def shift(x, axis, n, by):
@@ -375,7 +384,8 @@
     strip = both[0] + swap_y(both[1].astype(BF)).astype(F32)
     mine, z = reduce_z(strip, cols, z)
     z = lax.all_to_all(z, "col", 0, 0)
-    dq, dk, dv, dg = merge(y, z, g, c)
+    dq, dg = merge(y, g.shape, g, c)
+    dk, dv = merge(z, g.shape)
     mine = mine.T
     wf = weight.astype(F32)
     every = [mine] + [shift(mine, "head", HEADS, s) for s in range(1, HEADS)]

time: 158 us -> 156 us (0.987)
    unnamed x25 -> x23, local copies, waits for them, and re-layouts: 3.4 us -> 2.75 us
  transfers between devices with their start and end apart: 25 -> 25, of which waited for: 15 -> 15; matrix products, arithmetic and copies ran while one was open for 6% -> 6% of each run, Pallas kernels for 21% -> 22%
where the time goes in v2:
time: 156 us
  waiting for transfers between devices  52.9 us (34%)
  starting transfers between devices  52.3 us (34%)
  Pallas kernels  35.1 us (22%)
  other arithmetic  6.11 us (4%)
  local copies, waits for them, and re-layouts  4.3 us (3%)
  matrix products  4.09 us (3%)
    pallas_call x3, Pallas kernels, attend(): pl.pallas_call(functools.partial(attend_kernel, ts, first, last, len(extr...  30.4 us
    ppermute x14, waiting for transfers between devices, shift(): return lax.ppermute(x, axis, [(i, (i + by) % n) for i in range(n)])  30.2 us
    ppermute x14, starting transfers between devices, shift(): return lax.ppermute(x, axis, [(i, (i + by) % n) for i in range(n)])  21.8 us
    ppermute x6, starting transfers between devices, shift_x(): lax.ppermute(x, 'row', [(r, r // 4 * 4 + (r + by) % 4) for r in range(8)])  12.7 us
    ppermute x6, waiting for transfers between devices, shift_x(): lax.ppermute(x, 'row', [(r, r // 4 * 4 + (r + by) % 4) for r in range(8)])  8.51 us
    ppermute x2, waiting for transfers between devices, swap_y(): return lax.ppermute(x, 'row', [(r, (r + 4) % 8) for r in range(8)])  7.61 us
    all_to_all x1, starting transfers between devices, body(): z = lax.all_to_all(z, 'col', 0, 0)  5.31 us
    ppermute x2, starting transfers between devices, swap_y(): return lax.ppermute(x, 'row', [(r, (r + 4) % 8) for r in range(8)])  4.76 us
  transfers between devices with their start and end apart: 25, of which 15 were waited for; matrix products, arithmetic and copies ran while one was open for 6% of the time, Pallas kernels for 22%

profile of v2, /device:TPU:8, one launch (start us, length us, event | category | flops | bytes accessed | tf_op | source)
XLA Modules:
  0.0 155.8 jit_solution(14799152459966368008)
XLA Ops:
  0.7 2.0 %fusion = f32[4,128,128]{2,0,1:T(4,128)S(1)} fusion(bf16[32,4]{0,1:T(4,128)(2,1)} %param.14, bf16[4,8,128,128]{3,2,1,0:T(8,128)(2,1)} %bitcast.93), kind=kOutput, calls=%fused_computation.3 | convolution fusion | flops 4194304 | bytes 1310976 | tf_op jit(solution)/shard_map/dot_general | solution.py:357
  3.3 2.3 %collective-permute-start.1 = (f32[128,128]{0,1:T(8,128)S(1)}, f32[128,128]{0,1:T(8,128)S(1)}, u32[]{:S(2)}, u32[]{:S(2)}) collective-permute-start(f32[128,128]{0,1:T(8,128)S(1)} %bitcast.91), channel_id=1, source_target_pairs={{0,2},{1,3},{2,0},{3,1},{4,6},{5,7},{6,4},{7,5},{8,10},{9,11},{10,... | collective-permute-start | bytes 196616 | tf_op jit(solution)/shard_map/ppermute | solution.py:319
  6.0 3.2 %collective-permute-done.1 = f32[128,128]{0,1:T(8,128)S(1)} collective-permute-done((f32[128,128]{0,1:T(8,128)S(1)}, f32[128,128]{0,1:T(8,128)S(1)}, u32[]{:S(2)}, u32[]{:S(2)}) %collective-permute-start.1) | collective-permute-done | bytes 65568 | tf_op jit(solution)/shard_map/ppermute | solution.py:319
  9.7 6.1 %collective-permute-start.4 = (f16[128,128]{1,0:T(8,128)(2,1)S(1)}, f16[128,128]{1,0:T(8,128)(2,1)S(1)}, u32[]{:S(2)}, u32[]{:S(2)}) collective-permute-start(f16[128,128]{1,0:T(8,128)(2,1)S(1)} %bitcast.78), channel_id=1, source_target_pairs={{0,20},{4,24},{8,28},{12,0},{16,4},{20,8},{24,12},{28,16},{1,21},{... | collective-permute-start | bytes 98312 | tf_op jit(solution)/shard_map/ppermute | solution.py:319
  15.9 2.0 %shard_map.119 = bf16[8,5,4,32,128]{4,3,2,1,0:T(8,128)(2,1)} custom-call(bf16[1,32,40,128]{3,2,1,0:T(8,128)(2,1)S(1)} %copy-done.3, bf16[1,32,40,128]{3,2,1,0:T(8,128)(2,1)S(1)} %copy-done.4, bf16[1,32,40,128]{3,2,1,0:T(8,128)(2,1)S(1)} %copy-done.5, bf16[1,32,40,128]{3,2,1,0:T(8,128)(2,1)S(1)} %copy-done, bf16[1,32,40,128]{3,2,1,0:T(8,128)(2,1)S(1)} %copy-done.1), custom_call_target="tpu_custom_call" | custom-call | tf_op jit(solution)/shard_map/pallas_call | solution.py:296
  17.8 4.9 %collective-permute-done.3 = f16[128,128]{1,0:T(8,128)(2,1)S(1)} collective-permute-done((f16[128,128]{1,0:T(8,128)(2,1)S(1)}, f16[128,128]{1,0:T(8,128)(2,1)S(1)}, u32[]{:S(2)}, u32[]{:S(2)}) %collective-permute-start.3) | collective-permute-done | bytes 32800 | tf_op jit(solution)/shard_map/ppermute | solution.py:319
  23.9 2.3 %collective-permute-start.6 = (f16[2,128,128]{2,1,0:T(8,128)(2,1)S(1)}, f16[2,128,128]{2,1,0:T(8,128)(2,1)S(1)}, u32[]{:S(2)}, u32[]{:S(2)}) collective-permute-start(f16[2,128,128]{2,1,0:T(8,128)(2,1)S(1)} %pad_maximum_fusion.3), channel_id=1, source_target_pairs={{0,28},{4,0},{8,4},{12,8},{16,12},{20,16},{24,20},{28,24},{1,29},{... | collective-permute-start | bytes 196616 | tf_op jit(solution)/shard_map/ppermute | solution.py:319
  26.2 2.5 %collective-permute-done.5 = f16[3,128,128]{2,1,0:T(8,128)(2,1)S(1)} collective-permute-done((f16[3,128,128]{2,1,0:T(8,128)(2,1)S(1)}, f16[3,128,128]{2,1,0:T(8,128)(2,1)S(1)}, u32[]{:S(2)}, u32[]{:S(2)}) %collective-permute-start.5) | collective-permute-done | bytes 98336 | tf_op jit(solution)/shard_map/ppermute | solution.py:319
  28.9 4.2 %all-to-all-start = ((bf16[8,5,4,32,128]{4,3,2,1,0:T(8,128)(2,1)}), bf16[8,5,4,32,128]{4,3,2,1,0:T(8,128)(2,1)S(1)}, u32[]{:S(2)}, u32[]{:S(2)}) async-start(bf16[8,5,4,32,128]{4,3,2,1,0:T(8,128)(2,1)} %shard_map.119), calls=%async_computation | async-start | bytes 2621440 | tf_op jit(solution)/shard_map/all_to_all | solution.py:371
  33.1 2.4 %collective-permute-start.7 = (f16[8,128,128]{2,1,0:T(8,128)(2,1)S(1)}, f16[8,128,128]{2,1,0:T(8,128)(2,1)S(1)}, u32[]{:S(2)}, u32[]{:S(2)}) collective-permute-start(f16[8,128,128]{2,1,0:T(8,128)(2,1)S(1)} %slice_dynamic-update-slice_fusion), channel_id=1, source_target_pairs={{0,128},{32,160},{64,192},{96,224},{128,0},{160,32},{192,64},{224,... | collective-permute-start | bytes 786440 | tf_op jit(solution)/shard_map/ppermute | solution.py:327
  35.5 5.6 %collective-permute-done.7 = f16[8,128,128]{2,1,0:T(8,128)(2,1)S(1)} collective-permute-done((f16[8,128,128]{2,1,0:T(8,128)(2,1)S(1)}, f16[8,128,128]{2,1,0:T(8,128)(2,1)S(1)}, u32[]{:S(2)}, u32[]{:S(2)}) %collective-permute-start.7) | collective-permute-done | bytes 262176 | tf_op jit(solution)/shard_map/ppermute | solution.py:327
  42.1 3.0 %collective-permute-start.10 = (f16[2,8,128,128]{3,2,1,0:T(8,128)(2,1)}, f16[2,8,128,128]{3,2,1,0:T(8,128)(2,1)}, u32[]{:S(2)}, u32[]{:S(2)}) collective-permute-start(f16[2,8,128,128]{3,2,1,0:T(8,128)(2,1)} %get-tuple-element.79), channel_id=1, source_target_pairs={{0,64},{32,96},{64,0},{96,32},{128,192},{160,224},{192,128},{224,1... | collective-permute-start | bytes 1572872 | tf_op jit(solution)/shard_map/ppermute | solution.py:323
  45.7 2.6 %collective-permute-start.9 = (f16[2,8,128,128]{3,2,1,0:T(8,128)(2,1)}, f16[2,8,128,128]{3,2,1,0:T(8,128)(2,1)}, u32[]{:S(2)}, u32[]{:S(2)}) collective-permute-start(f16[2,8,128,128]{3,2,1,0:T(8,128)(2,1)} %get-tuple-element.79), channel_id=1, source_target_pairs={{0,96},{32,0},{64,32},{96,64},{128,224},{160,128},{192,160},{224,1... | collective-permute-start | bytes 1572872 | tf_op jit(solution)/shard_map/ppermute | solution.py:323
  49.7 8.5 %collective-permute-done.10 = f16[2,8,128,128]{3,2,1,0:T(8,128)(2,1)} collective-permute-done((f16[2,8,128,128]{3,2,1,0:T(8,128)(2,1)}, f16[2,8,128,128]{3,2,1,0:T(8,128)(2,1)}, u32[]{:S(2)}, u32[]{:S(2)}) %collective-permute-start.10) | collective-permute-done | bytes 524320 | tf_op jit(solution)/shard_map/ppermute | solution.py:323
  58.2 2.1 %convert_element_type.67.refs_2_ = f32[2,8,128,128]{3,2,1,0:T(8,128)} convert(f16[2,8,128,128]{3,2,1,0:T(8,128)(2,1)} %collective-permute-done.10) | non-fusion elementwise | flops 262144 | bytes 1572864 | tf_op jit(solution)/shard_map/convert_element_type | solution.py:375
  60.3 3.5 %all-to-all-done.refs_1_ = bf16[8,5,4,32,128]{4,3,2,1,0:T(8,128)(2,1)S(1)} async-done(((bf16[8,5,4,32,128]{4,3,2,1,0:T(8,128)(2,1)}), bf16[8,5,4,32,128]{4,3,2,1,0:T(8,128)(2,1)S(1)}, u32[]{:S(2)}, u32[]{:S(2)}) %all-to-all-start) | async-done | bytes 1310752 | tf_op jit(solution)/shard_map/all_to_all | solution.py:371
  65.1 8.8 %shard_map.120 = (bf16[8,5,2,32,128]{4,3,2,1,0:T(8,128)(2,1)S(1)}, bf16[2,8,128,128]{3,2,1,0:T(8,128)(2,1)S(1)}, bf16[5,1024,128]{2,1,0:T(8,128)(2,1)S(1)}, bf16...) custom-call(s32[10]{0:T(128)S(1)} %pad_add_fusion.refs_0_, bf16[8,5,4,32,128]{4,3,2,1,0:T(8,128)(2,1)S(1)} %all-to-all-done.refs_1_, ...), custom_call_target="tpu_custom_call" | custom-call | flops 2000000000 | bytes 8000000 | tf_op jit(solution)/shard_map/pallas_call | solution.py:262
  75.1 3.1 %collective-permute-start.11 = (bf16[2,8,128,128]{3,2,1,0:T(8,128)(2,1)S(1)}, bf16[2,8,128,128]{3,2,1,0:T(8,128)(2,1)S(1)}, u32[]{:S(2)}, u32[]{:S(2)}) collective-permute-start(bf16[2,8,128,128]{3,2,1,0:T(8,128)(2,1)S(1)} %get-tuple-element.50), channel_id=1, source_target_pairs={{0,64},{32,96},{64,0},{96,32},{128,192},{160,224},{192,128},{224,1... | collective-permute-start | bytes 1572872 | tf_op jit(solution)/shard_map/ppermute | solution.py:323
  78.2 12.2 %shard_map.121 = (bf16[8,5,2,32,128]{4,3,2,1,0:T(8,128)(2,1)S(1)}, bf16[2,8,128,128]{3,2,1,0:T(8,128)(2,1)S(1)}, bf16[2,8,128,128]{3,2,1,0:T(8,128)(2,1)S(1)}, b...) custom-call(s32[10]{0:T(128)S(1)} %pad_add_fusion.refs_0_, ...), custom_call_target="tpu_custom_call" | custom-call | flops 4000000000 | bytes 8000000 | tf_op jit(solution)/shard_map/pallas_call | solution.py:262
  91.1 2.7 %collective-permute-start.12 = (bf16[2,8,128,128]{3,2,1,0:T(8,128)(2,1)S(1)}, bf16[2,8,128,128]{3,2,1,0:T(8,128)(2,1)S(1)}, u32[]{:S(2)}, u32[]{:S(2)}) collective-permute-start(bf16[2,8,128,128]{3,2,1,0:T(8,128)(2,1)S(1)} %get-tuple-element.54), channel_id=1, source_target_pairs={{0,96},{32,0},{64,32},{96,64},{128,224},{160,128},{192,160},{224,1... | collective-permute-start | bytes 1572872 | tf_op jit(solution)/shard_map/ppermute | solution.py:323
  93.7 9.4 %shard_map.122 = (bf16[8,5,2,32,128]{4,3,2,1,0:T(8,128)(2,1)}, bf16[8,5,2,32,128]{4,3,2,1,0:T(8,128)(2,1)}, f32[2,8,128,128]{3,2,1,0:T(8,128)S(1)}) custom-call(s32[10]{0:T(128)S(1)} %pad_add_fusion.refs_0_, bf16[8,5,4,32,128]{4,3,2,1,0:T(8,128)(2,1)S(1)} %all-to-all-done.refs_1_, f32[2,8,128,128]{3,2,1,0:T(8,128)S(1)} %get-tuple-element.80.refs_2_, ...), custom_call_target="tpu_custom_call" | custom-call | flops 2000000000 | bytes 8000000 | tf_op jit(solution)/shard_map/pallas_call | solution.py:262
  103.4 2.4 %collective-permute-start.14 = (bf16[8,128,128]{2,1,0:T(8,128)(2,1)S(1)}, bf16[8,128,128]{2,1,0:T(8,128)(2,1)S(1)}, u32[]{:S(2)}, u32[]{:S(2)}) collective-permute-start(bf16[8,128,128]{2,1,0:T(8,128)(2,1)S(1)} %fusion.4), channel_id=1, source_target_pairs={{0,128},{32,160},{64,192},{96,224},{128,0},{160,32},{192,64},{224,... | collective-permute-start | bytes 786440 | tf_op jit(solution)/shard_map/ppermute | solution.py:327
  105.8 3.5 %all-to-all-start.1 = ((bf16[8,5,2,32,128]{4,3,2,1,0:T(8,128)(2,1)}), bf16[8,5,2,32,128]{4,3,2,1,0:T(8,128)(2,1)S(1)}, u32[]{:S(2)}, u32[]{:S(2)}) async-start(bf16[8,5,2,32,128]{4,3,2,1,0:T(8,128)(2,1)} %get-tuple-element.51), calls=%async_computation.1 | async-start | bytes 1310720 | tf_op jit(solution)/shard_map/all_to_all | solution.py:382
  109.3 2.0 %collective-permute-done.14 = bf16[8,128,128]{2,1,0:T(8,128)(2,1)S(1)} collective-permute-done((bf16[8,128,128]{2,1,0:T(8,128)(2,1)S(1)}, bf16[8,128,128]{2,1,0:T(8,128)(2,1)S(1)}, u32[]{:S(2)}, u32[]{:S(2)}) %collective-permute-start.14) | collective-permute-done | bytes 262176 | tf_op jit(solution)/shard_map/ppermute | solution.py:327
  113.7 8.8 %collective-permute-done.16 = bf16[2,128,128]{2,1,0:T(8,128)(2,1)S(1)} collective-permute-done((bf16[2,128,128]{2,1,0:T(8,128)(2,1)S(1)}, bf16[2,128,128]{2,1,0:T(8,128)(2,1)S(1)}, u32[]{:S(2)}, u32[]{:S(2)}) %collective-permute-start.16) | collective-permute-done | bytes 65568 | tf_op jit(solution)/shard_map/ppermute | solution.py:319
  123.7 3.9 %collective-permute-start.17 = (bf16[128,128]{1,0:T(8,128)(2,1)S(1)}, bf16[128,128]{1,0:T(8,128)(2,1)S(1)}, u32[]{:S(2)}, u32[]{:S(2)}) collective-permute-start(bf16[128,128]{1,0:T(8,128)(2,1)S(1)} %get-tuple-element.78), channel_id=1, source_target_pairs={{0,20},{4,24},{8,28},{12,0},{16,4},{20,8},{24,12},{28,16},{1,21},{... | collective-permute-start | bytes 98312 | tf_op jit(solution)/shard_map/ppermute | solution.py:319
  130.9 3.7 %collective-permute-done.18 = bf16[128,128]{1,0:T(8,128)(2,1)S(1)} collective-permute-done((bf16[128,128]{1,0:T(8,128)(2,1)S(1)}, bf16[128,128]{1,0:T(8,128)(2,1)S(1)}, u32[]{:S(2)}, u32[]{:S(2)}) %collective-permute-start.18) | collective-permute-done | bytes 32800 | tf_op jit(solution)/shard_map/ppermute | solution.py:319
  134.6 5.3 %all-to-all-start.2 = ((bf16[8,5,2,32,128]{4,3,2,1,0:T(8,128)(2,1)}), bf16[8,5,2,32,128]{4,3,2,1,0:T(8,128)(2,1)S(1)}, u32[]{:S(2)}, u32[]{:S(2)}) async-start(bf16[8,5,2,32,128]{4,3,2,1,0:T(8,128)(2,1)} %get-tuple-element.57), calls=%async_computation.2 | async-start | bytes 1310720 | tf_op jit(solution)/shard_map/all_to_all | solution.py:386
  140.6 1.8 %collective-permute-start.20 = (f32[128,128]{0,1:T(8,128)S(1)}, f32[128,128]{0,1:T(8,128)S(1)}, u32[]{:S(2)}, u32[]{:S(2)}) collective-permute-start(f32[128,128]{0,1:T(8,128)S(1)} %fusion.14), channel_id=1, source_target_pairs={{0,2},{1,3},{2,0},{3,1},{4,6},{5,7},{6,4},{7,5},{8,10},{9,11},{10,... | collective-permute-start | bytes 196616 | tf_op jit(solution)/shard_map/ppermute | solution.py:319
  142.9 3.3 %collective-permute-done.20 = f32[128,128]{0,1:T(8,128)S(1)} collective-permute-done((f32[128,128]{0,1:T(8,128)S(1)}, f32[128,128]{0,1:T(8,128)S(1)}, u32[]{:S(2)}, u32[]{:S(2)}) %collective-permute-start.20) | collective-permute-done | bytes 65568 | tf_op jit(solution)/shard_map/ppermute | solution.py:319
  146.7 2.1 %convolution_convert_fusion = bf16[32,128,128]{2,0,1:T(8,128)(2,1)S(1)} fusion(f32[1,16384]{1,0:T(1,128)S(1)} %bitcast.85, f32[1,16384]{1,0:T(1,128)S(1)} %bitcast.86, f32[1,16384]{1,0:T(1,128)S(1)} %bitcast.87, f32[1,16384]{1,0:T(1,128)S(1)} %bitcast.84, f32[4,32]{1,0:T(4,128)S(1)} %gather_fusion, pred[4]{0:T(512)(128)(4,1)S(1)} %compare_and_fusion), kind=kOutput, calls=%fused_computation.1 | convolution fusion | flops 25886848 | bytes 1311236 | tf_op jit(solution)/shard_map/dot_general | solution.py:394
  151.6 3.1 %all-to-all-done.2.x_ref = bf16[8,5,2,32,128]{4,3,2,1,0:T(8,128)(2,1)S(1)} async-done(((bf16[8,5,2,32,128]{4,3,2,1,0:T(8,128)(2,1)}), bf16[8,5,2,32,128]{4,3,2,1,0:T(8,128)(2,1)S(1)}, u32[]{:S(2)}, u32[]{:S(2)}) %all-to-all-start.2) | async-done | bytes 655392 | tf_op jit(solution)/shard_map/all_to_all | solution.py:386
  (86 shorter events, 21.3 us)
Async XLA Ops:
  0.7 15.1 %copy-start = (bf16[1,32,40,128]{3,2,1,0:T(8,128)(2,1)S(1)}, bf16[1,32,40,128]{3,2,1,0:T(8,128)(2,1)}, u32[]{:S(2)}) copy-start(bf16[1,32,40,128]{3,2,1,0:T(8,128)(2,1)} %g_ref.3) | copy-start | bytes 983044
  0.7 15.1 %copy-start.1 = (bf16[1,32,40,128]{3,2,1,0:T(8,128)(2,1)S(1)}, bf16[1,32,40,128]{3,2,1,0:T(8,128)(2,1)}, u32[]{:S(2)}) copy-start(bf16[1,32,40,128]{3,2,1,0:T(8,128)(2,1)} %c_ref.3) | copy-start | bytes 983044
  0.7 15.1 %copy-start.3 = (bf16[1,32,40,128]{3,2,1,0:T(8,128)(2,1)S(1)}, bf16[1,32,40,128]{3,2,1,0:T(8,128)(2,1)}, u32[]{:S(2)}) copy-start(bf16[1,32,40,128]{3,2,1,0:T(8,128)(2,1)} %q_ref.1) | copy-start | bytes 983044
  0.7 15.1 %copy-start.4 = (bf16[1,32,40,128]{3,2,1,0:T(8,128)(2,1)S(1)}, bf16[1,32,40,128]{3,2,1,0:T(8,128)(2,1)}, u32[]{:S(2)}) copy-start(bf16[1,32,40,128]{3,2,1,0:T(8,128)(2,1)} %k_ref.1) | copy-start | bytes 983044
  0.7 15.1 %copy-start.5 = (bf16[1,32,40,128]{3,2,1,0:T(8,128)(2,1)S(1)}, bf16[1,32,40,128]{3,2,1,0:T(8,128)(2,1)}, u32[]{:S(2)}) copy-start(bf16[1,32,40,128]{3,2,1,0:T(8,128)(2,1)} %v_ref.1) | copy-start | bytes 983044
  3.1 2.9 %collective-permute-start.2 = (f32[128,128]{0,1:T(8,128)S(1)}, f32[128,128]{0,1:T(8,128)S(1)}, u32[]{:S(2)}, u32[]{:S(2)}) collective-permute-start(f32[128,128]{0,1:T(8,128)S(1)} %bitcast.90), channel_id=1, source_target_pairs={{0,3},{1,0},{2,1},{3,2},{4,7},{5,4},{6,5},{7,6},{8,11},{9,8},{10,9... | collective-permute-start | bytes 196616 | tf_op jit(solution)/shard_map/ppermute | solution.py:319
  3.3 6.0 %collective-permute-start.1 = (f32[128,128]{0,1:T(8,128)S(1)}, f32[128,128]{0,1:T(8,128)S(1)}, u32[]{:S(2)}, u32[]{:S(2)}) collective-permute-start(f32[128,128]{0,1:T(8,128)S(1)} %bitcast.91), channel_id=1, source_target_pairs={{0,2},{1,3},{2,0},{3,1},{4,6},{5,7},{6,4},{7,5},{8,10},{9,11},{10,... | collective-permute-start | bytes 196616 | tf_op jit(solution)/shard_map/ppermute | solution.py:319
  5.6 4.1 %collective-permute-start = (f32[128,128]{0,1:T(8,128)S(1)}, f32[128,128]{0,1:T(8,128)S(1)}, u32[]{:S(2)}, u32[]{:S(2)}) collective-permute-start(f32[128,128]{0,1:T(8,128)S(1)} %bitcast.92), channel_id=1, source_target_pairs={{0,1},{1,2},{2,3},{3,0},{4,5},{5,6},{6,7},{7,4},{8,9},{9,10},{10,1... | collective-permute-start | bytes 196616 | tf_op jit(solution)/shard_map/ppermute | solution.py:319
  9.7 8.1 %collective-permute-start.4 = (f16[128,128]{1,0:T(8,128)(2,1)S(1)}, f16[128,128]{1,0:T(8,128)(2,1)S(1)}, u32[]{:S(2)}, u32[]{:S(2)}) collective-permute-start(f16[128,128]{1,0:T(8,128)(2,1)S(1)} %bitcast.78), channel_id=1, source_target_pairs={{0,20},{4,24},{8,28},{12,0},{16,4},{20,8},{24,12},{28,16},{1,21},{... | collective-permute-start | bytes 98312 | tf_op jit(solution)/shard_map/ppermute | solution.py:319
  15.8 7.0 %collective-permute-start.3 = (f16[128,128]{1,0:T(8,128)(2,1)S(1)}, f16[128,128]{1,0:T(8,128)(2,1)S(1)}, u32[]{:S(2)}, u32[]{:S(2)}) collective-permute-start(f16[128,128]{1,0:T(8,128)(2,1)S(1)} %bitcast.79), channel_id=1, source_target_pairs={{0,12},{4,16},{8,20},{12,24},{16,28},{20,0},{24,4},{28,8},{1,13},{... | collective-permute-start | bytes 98312 | tf_op jit(solution)/shard_map/ppermute | solution.py:319
  22.8 5.9 %collective-permute-start.5 = (f16[3,128,128]{2,1,0:T(8,128)(2,1)S(1)}, f16[3,128,128]{2,1,0:T(8,128)(2,1)S(1)}, u32[]{:S(2)}, u32[]{:S(2)}) collective-permute-start(f16[3,128,128]{2,1,0:T(8,128)(2,1)S(1)} %pad_maximum_fusion.1), channel_id=1, source_target_pairs={{0,4},{4,8},{8,12},{12,16},{16,20},{20,24},{24,28},{28,0},{1,5},{5... | collective-permute-start | bytes 294920 | tf_op jit(solution)/shard_map/ppermute | solution.py:319
  23.9 4.8 %collective-permute-start.6 = (f16[2,128,128]{2,1,0:T(8,128)(2,1)S(1)}, f16[2,128,128]{2,1,0:T(8,128)(2,1)S(1)}, u32[]{:S(2)}, u32[]{:S(2)}) collective-permute-start(f16[2,128,128]{2,1,0:T(8,128)(2,1)S(1)} %pad_maximum_fusion.3), channel_id=1, source_target_pairs={{0,28},{4,0},{8,4},{12,8},{16,12},{20,16},{24,20},{28,24},{1,29},{... | collective-permute-start | bytes 196616 | tf_op jit(solution)/shard_map/ppermute | solution.py:319
  28.9 34.9 %all-to-all-start = ((bf16[8,5,4,32,128]{4,3,2,1,0:T(8,128)(2,1)}), bf16[8,5,4,32,128]{4,3,2,1,0:T(8,128)(2,1)S(1)}, u32[]{:S(2)}, u32[]{:S(2)}) async-start(bf16[8,5,4,32,128]{4,3,2,1,0:T(8,128)(2,1)} %shard_map.119), calls=%async_computation | async-start | bytes 2621440 | tf_op jit(solution)/shard_map/all_to_all | solution.py:371
  33.1 15.2 %copy-start.7 = (s32[8]{0:T(128)S(1)}, s32[8]{0:T(128)}, u32[]{:S(2)}) copy-start(s32[8]{0:T(128)} %param.15) | copy-start | bytes 100
  33.1 8.0 %collective-permute-start.7 = (f16[8,128,128]{2,1,0:T(8,128)(2,1)S(1)}, f16[8,128,128]{2,1,0:T(8,128)(2,1)S(1)}, u32[]{:S(2)}, u32[]{:S(2)}) collective-permute-start(f16[8,128,128]{2,1,0:T(8,128)(2,1)S(1)} %slice_dynamic-update-slice_fusion), channel_id=1, source_target_pairs={{0,128},{32,160},{64,192},{96,224},{128,0},{160,32},{192,64},{224,... | collective-permute-start | bytes 786440 | tf_op jit(solution)/shard_map/ppermute | solution.py:327
  42.1 16.1 %collective-permute-start.10 = (f16[2,8,128,128]{3,2,1,0:T(8,128)(2,1)}, f16[2,8,128,128]{3,2,1,0:T(8,128)(2,1)}, u32[]{:S(2)}, u32[]{:S(2)}) collective-permute-start(f16[2,8,128,128]{3,2,1,0:T(8,128)(2,1)} %get-tuple-element.79), channel_id=1, source_target_pairs={{0,64},{32,96},{64,0},{96,32},{128,192},{160,224},{192,128},{224,1... | collective-permute-start | bytes 1572872 | tf_op jit(solution)/shard_map/ppermute | solution.py:323
  45.1 28.7 %collective-permute-start.8 = (f16[2,8,128,128]{3,2,1,0:T(8,128)(2,1)}, f16[2,8,128,128]{3,2,1,0:T(8,128)(2,1)S(1)}, u32[]{:S(2)}, u32[]{:S(2)}) collective-permute-start(f16[2,8,128,128]{3,2,1,0:T(8,128)(2,1)} %get-tuple-element.79), channel_id=1, source_target_pairs={{0,32},{32,64},{64,96},{96,0},{128,160},{160,192},{192,224},{224,1... | collective-permute-start | bytes 1572872 | tf_op jit(solution)/shard_map/ppermute | solution.py:323
  45.7 28.2 %collective-permute-start.9 = (f16[2,8,128,128]{3,2,1,0:T(8,128)(2,1)}, f16[2,8,128,128]{3,2,1,0:T(8,128)(2,1)}, u32[]{:S(2)}, u32[]{:S(2)}) collective-permute-start(f16[2,8,128,128]{3,2,1,0:T(8,128)(2,1)} %get-tuple-element.79), channel_id=1, source_target_pairs={{0,96},{32,0},{64,32},{96,64},{128,224},{160,128},{192,160},{224,1... | collective-permute-start | bytes 1572872 | tf_op jit(solution)/shard_map/ppermute | solution.py:323
  75.1 18.6 %collective-permute-start.11 = (bf16[2,8,128,128]{3,2,1,0:T(8,128)(2,1)S(1)}, bf16[2,8,128,128]{3,2,1,0:T(8,128)(2,1)S(1)}, u32[]{:S(2)}, u32[]{:S(2)}) collective-permute-start(bf16[2,8,128,128]{3,2,1,0:T(8,128)(2,1)S(1)} %get-tuple-element.50), channel_id=1, source_target_pairs={{0,64},{32,96},{64,0},{96,32},{128,192},{160,224},{192,128},{224,1... | collective-permute-start | bytes 1572872 | tf_op jit(solution)/shard_map/ppermute | solution.py:323
  90.4 12.8 %collective-permute-start.13 = (bf16[2,8,128,128]{3,2,1,0:T(8,128)(2,1)S(1)}, bf16[2,8,128,128]{3,2,1,0:T(8,128)(2,1)S(1)}, u32[]{:S(2)}, u32[]{:S(2)}) collective-permute-start(bf16[2,8,128,128]{3,2,1,0:T(8,128)(2,1)S(1)} %get-tuple-element.55), channel_id=1, source_target_pairs={{0,32},{32,64},{64,96},{96,0},{128,160},{160,192},{192,224},{224,1... | collective-permute-start | bytes 1572872 | tf_op jit(solution)/shard_map/ppermute | solution.py:323
  91.1 12.1 %collective-permute-start.12 = (bf16[2,8,128,128]{3,2,1,0:T(8,128)(2,1)S(1)}, bf16[2,8,128,128]{3,2,1,0:T(8,128)(2,1)S(1)}, u32[]{:S(2)}, u32[]{:S(2)}) collective-permute-start(bf16[2,8,128,128]{3,2,1,0:T(8,128)(2,1)S(1)} %get-tuple-element.54), channel_id=1, source_target_pairs={{0,96},{32,0},{64,32},{96,64},{128,224},{160,128},{192,160},{224,1... | collective-permute-start | bytes 1572872 | tf_op jit(solution)/shard_map/ppermute | solution.py:323
  103.4 8.0 %collective-permute-start.14 = (bf16[8,128,128]{2,1,0:T(8,128)(2,1)S(1)}, bf16[8,128,128]{2,1,0:T(8,128)(2,1)S(1)}, u32[]{:S(2)}, u32[]{:S(2)}) collective-permute-start(bf16[8,128,128]{2,1,0:T(8,128)(2,1)S(1)} %fusion.4), channel_id=1, source_target_pairs={{0,128},{32,160},{64,192},{96,224},{128,0},{160,32},{192,64},{224,... | collective-permute-start | bytes 786440 | tf_op jit(solution)/shard_map/ppermute | solution.py:327
  105.8 28.9 %all-to-all-start.1 = ((bf16[8,5,2,32,128]{4,3,2,1,0:T(8,128)(2,1)}), bf16[8,5,2,32,128]{4,3,2,1,0:T(8,128)(2,1)S(1)}, u32[]{:S(2)}, u32[]{:S(2)}) async-start(bf16[8,5,2,32,128]{4,3,2,1,0:T(8,128)(2,1)} %get-tuple-element.51), calls=%async_computation.1 | async-start | bytes 1310720 | tf_op jit(solution)/shard_map/all_to_all | solution.py:382
  111.5 28.5 %copy-start.6 = (bf16[32,4]{0,1:T(4,128)(2,1)S(1)}, bf16[32,4]{0,1:T(4,128)(2,1)}, u32[]{:S(2)}) copy-start(bf16[32,4]{0,1:T(4,128)(2,1)} %param.14) | copy-start | bytes 772
  111.5 12.2 %collective-permute-start.15 = (bf16[3,128,128]{2,1,0:T(8,128)(2,1)S(1)}, bf16[3,128,128]{2,1,0:T(8,128)(2,1)S(1)}, u32[]{:S(2)}, u32[]{:S(2)}) collective-permute-start(bf16[3,128,128]{2,1,0:T(8,128)(2,1)S(1)} %pad_maximum_fusion.2), channel_id=1, source_target_pairs={{0,28},{4,0},{8,4},{12,8},{16,12},{20,16},{24,20},{28,24},{1,29},{... | collective-permute-start | bytes 294920 | tf_op jit(solution)/shard_map/ppermute | solution.py:319
  112.7 9.8 %collective-permute-start.16 = (bf16[2,128,128]{2,1,0:T(8,128)(2,1)S(1)}, bf16[2,128,128]{2,1,0:T(8,128)(2,1)S(1)}, u32[]{:S(2)}, u32[]{:S(2)}) collective-permute-start(bf16[2,128,128]{2,1,0:T(8,128)(2,1)S(1)} %pad_maximum_fusion.4), channel_id=1, source_target_pairs={{0,4},{4,8},{8,12},{12,16},{16,20},{20,24},{24,28},{28,0},{1,5},{5... | collective-permute-start | bytes 196616 | tf_op jit(solution)/shard_map/ppermute | solution.py:319
  123.7 7.2 %collective-permute-start.17 = (bf16[128,128]{1,0:T(8,128)(2,1)S(1)}, bf16[128,128]{1,0:T(8,128)(2,1)S(1)}, u32[]{:S(2)}, u32[]{:S(2)}) collective-permute-start(bf16[128,128]{1,0:T(8,128)(2,1)S(1)} %get-tuple-element.78), channel_id=1, source_target_pairs={{0,20},{4,24},{8,28},{12,0},{16,4},{20,8},{24,12},{28,16},{1,21},{... | collective-permute-start | bytes 98312 | tf_op jit(solution)/shard_map/ppermute | solution.py:319
  127.7 6.9 %collective-permute-start.18 = (bf16[128,128]{1,0:T(8,128)(2,1)S(1)}, bf16[128,128]{1,0:T(8,128)(2,1)S(1)}, u32[]{:S(2)}, u32[]{:S(2)}) collective-permute-start(bf16[128,128]{1,0:T(8,128)(2,1)S(1)} %get-tuple-element.77), channel_id=1, source_target_pairs={{0,12},{4,16},{8,20},{12,24},{16,28},{20,0},{24,4},{28,8},{1,13},{... | collective-permute-start | bytes 98312 | tf_op jit(solution)/shard_map/ppermute | solution.py:319
  134.6 20.0 %all-to-all-start.2 = ((bf16[8,5,2,32,128]{4,3,2,1,0:T(8,128)(2,1)}), bf16[8,5,2,32,128]{4,3,2,1,0:T(8,128)(2,1)S(1)}, u32[]{:S(2)}, u32[]{:S(2)}) async-start(bf16[8,5,2,32,128]{4,3,2,1,0:T(8,128)(2,1)} %get-tuple-element.57), calls=%async_computation.2 | async-start | bytes 1310720 | tf_op jit(solution)/shard_map/all_to_all | solution.py:386
  140.6 2.2 %collective-permute-start.21 = (f32[128,128]{0,1:T(8,128)S(1)}, f32[128,128]{0,1:T(8,128)S(1)}, u32[]{:S(2)}, u32[]{:S(2)}) collective-permute-start(f32[128,128]{0,1:T(8,128)S(1)} %fusion.14), channel_id=1, source_target_pairs={{0,3},{1,0},{2,1},{3,2},{4,7},{5,4},{6,5},{7,6},{8,11},{9,8},{10,9... | collective-permute-start | bytes 196616 | tf_op jit(solution)/shard_map/ppermute | solution.py:319
  140.6 5.5 %collective-permute-start.20 = (f32[128,128]{0,1:T(8,128)S(1)}, f32[128,128]{0,1:T(8,128)S(1)}, u32[]{:S(2)}, u32[]{:S(2)}) collective-permute-start(f32[128,128]{0,1:T(8,128)S(1)} %fusion.14), channel_id=1, source_target_pairs={{0,2},{1,3},{2,0},{3,1},{4,6},{5,7},{6,4},{7,5},{8,10},{9,11},{10,... | collective-permute-start | bytes 196616 | tf_op jit(solution)/shard_map/ppermute | solution.py:319
  142.5 4.1 %collective-permute-start.19 = (f32[128,128]{0,1:T(8,128)S(1)}, f32[128,128]{0,1:T(8,128)S(1)}, u32[]{:S(2)}, u32[]{:S(2)}) collective-permute-start(f32[128,128]{0,1:T(8,128)S(1)} %fusion.14), channel_id=1, source_target_pairs={{0,1},{1,2},{2,3},{3,0},{4,5},{5,6},{6,7},{7,4},{8,9},{9,10},{10,1... | collective-permute-start | bytes 196616 | tf_op jit(solution)/shard_map/ppermute | solution.py:319
  (1 other events, 1.2 us)

commit v3 on v2

--- a/solution.py
+++ b/solution.py
@@ -69,12 +69,9 @@
     (y_ref,) = take(1)
     z_ref = take(1)[0] if last else None
     db_refs = take(len(ts))
-    if last:
-        ka_out = vta_out = None
-        acc_out = None
-    else:
-        ka_out, vta_out, acc_out = take(3)
-    ka, vta, va, kk, s_ref, p_ref, acc, dbacc = refs
+    ka_out, vta_out = take(2) if first and not last else (None, None)
+    acc_out = None if last else take(1)[0]
+    va, kk, s_ref, p_ref, acc, dbacc = refs
     cols = x_ref.shape[0]
     row = pl.program_id(0)
     count = meta_ref[0]
@@ -84,6 +81,10 @@
     def _():
         dbacc[...] = jnp.zeros_like(dbacc)
 
+    if first:
+        ka_use, vta_use = ka_out.at[0], vta_out.at[0]
+    else:
+        ka_use, vta_use = ka_in.at[0], vta_in.at[0]
     ones16 = jnp.ones((16, BLK), BF)
     zeros48 = jnp.zeros((48, BLK), BF)
     lane = lax.broadcasted_iota(jnp.int32, (16, BLK), 1)
@@ -93,21 +94,16 @@
         val = x_ref[s, 0, 2]
         if first:
             mask = jnp.where(s * BLK + lane < count, 0.0, NEG).astype(BF)
-            ka[at, :] = jnp.concatenate([key, key, mask, zeros48], 0).T
-            vta[at, :] = jnp.concatenate([val, val, ones16, zeros48], 0).T
+            ka_use[at, :] = jnp.concatenate([key, key, mask, zeros48], 0).T
+            vta_use[at, :] = jnp.concatenate([val, val, ones16, zeros48], 0).T
         va[0:DIM, at] = val
         va[DIM : DIM + 16, at] = ones16
         kk[:, at] = key
     if first:
         acc[...] = jnp.zeros_like(acc)
-        ka_use, vta_use = ka, vta
     else:
         acc[...] = acc_in[0]
         y_ref[...] = y_in[...]
-        ka_use, vta_use = ka_in.at[0], vta_in.at[0]
-    if not last:
-        ka_out[0] = ka_use[...]
-        vta_out[0] = vta_use[...]
     sub = lax.broadcasted_iota(jnp.int32, (16, 2 * BLK), 0)
     unit = jnp.where(sub == 0, 1.0, 0.0).astype(BF)
     zero48 = jnp.zeros((48, 2 * BLK), BF)
@@ -257,8 +253,9 @@
     out_shape = [pairs] * (2 if last else 1)
     out_shape += [jax.ShapeDtypeStruct(tile_shape, F32 if last else BF)] * len(ts)
     if not last:
-        out_specs += [flat] * 3
-        out_shape += [jax.ShapeDtypeStruct(flat_shape, dt) for dt in (BF, BF, F32)]
+        new = (BF, BF, F32) if first else (F32,)
+        out_specs += [flat] * len(new)
+        out_shape += [jax.ShapeDtypeStruct(flat_shape, dt) for dt in new]
     outs = pl.pallas_call(
         functools.partial(attend_kernel, ts, first, last, len(extra)),
         grid=(rows,),
@@ -266,8 +263,6 @@
         out_specs=out_specs,
         out_shape=out_shape,
         scratch_shapes=[
-            pltpu.VMEM((wide, BLK), BF),
-            pltpu.VMEM((wide, BLK), BF),
             pltpu.VMEM((DIM + 16, wide), BF),
             pltpu.VMEM((DIM, wide), BF),
             pltpu.VMEM((len(ts), wide, 2 * BLK), F32),
@@ -285,7 +280,8 @@
     if last:
         return *outs[:2], dict(zip(ts, outs[2:])), None
     dbs, rest = outs[1 : 1 + len(ts)], outs[1 + len(ts) :]
-    return outs[0], dict(zip(ts, dbs)), (*rest, outs[0])
+    kept = () if first else tuple(state[:2])
+    return outs[0], dict(zip(ts, dbs)), (*kept, *rest, outs[0])
 
 
 VMEM_SPEC = pl.BlockSpec(memory_space=pltpu.VMEM)

time: 156 us -> 156 us (level)
  transfers between devices with their start and end apart: 25 -> 25, of which waited for: 15 -> 15; matrix products, arithmetic and copies ran while one was open for 6% -> 6% of each run, Pallas kernels for 22% -> 21%
where the time goes in v3:
time: 156 us; the launch traced here: 155 us
  waiting for transfers between devices  52.9 us (34%)
  starting transfers between devices  52.3 us (34%)
  Pallas kernels  34.6 us (22%)
  other arithmetic  6.11 us (4%)
  local copies, waits for them, and re-layouts  4.3 us (3%)
  matrix products  4.09 us (3%)
    ppermute x14, waiting for transfers between devices, shift(): return lax.ppermute(x, axis, [(i, (i + by) % n) for i in range(n)])  30.2 us
    pallas_call x3, Pallas kernels, attend(): pl.pallas_call(functools.partial(attend_kernel, ts, first, last, len(extr...  30 us
    ppermute x14, starting transfers between devices, shift(): return lax.ppermute(x, axis, [(i, (i + by) % n) for i in range(n)])  21.8 us
    ppermute x6, starting transfers between devices, shift_x(): lax.ppermute(x, 'row', [(r, r // 4 * 4 + (r + by) % 4) for r in range(8)])  12.7 us
    ppermute x6, waiting for transfers between devices, shift_x(): lax.ppermute(x, 'row', [(r, r // 4 * 4 + (r + by) % 4) for r in range(8)])  8.51 us
    ppermute x2, waiting for transfers between devices, swap_y(): return lax.ppermute(x, 'row', [(r, (r + 4) % 8) for r in range(8)])  7.62 us
    all_to_all x1, starting transfers between devices, body(): z = lax.all_to_all(z, 'col', 0, 0)  5.31 us
    ppermute x2, starting transfers between devices, swap_y(): return lax.ppermute(x, 'row', [(r, (r + 4) % 8) for r in range(8)])  4.76 us
  transfers between devices with their start and end apart: 25, of which 15 were waited for; matrix products, arithmetic and copies ran while one was open for 6% of the time, Pallas kernels for 21%

profile of v3, /device:TPU:8, one launch (start us, length us, event | category | flops | bytes accessed | tf_op | source)
XLA Modules:
  0.0 155.4 jit_solution(10666045927636248958)
XLA Ops:
  0.7 2.0 %fusion = f32[4,128,128]{2,0,1:T(4,128)S(1)} fusion(bf16[32,4]{0,1:T(4,128)(2,1)} %param.14, bf16[4,8,128,128]{3,2,1,0:T(8,128)(2,1)} %bitcast.93), kind=kOutput, calls=%fused_computation.3 | convolution fusion | flops 4194304 | bytes 1310976 | tf_op jit(solution)/shard_map/dot_general | solution.py:353
  3.3 2.3 %collective-permute-start.1 = (f32[128,128]{0,1:T(8,128)S(1)}, f32[128,128]{0,1:T(8,128)S(1)}, u32[]{:S(2)}, u32[]{:S(2)}) collective-permute-start(f32[128,128]{0,1:T(8,128)S(1)} %bitcast.91), channel_id=1, source_target_pairs={{0,2},{1,3},{2,0},{3,1},{4,6},{5,7},{6,4},{7,5},{8,10},{9,11},{10,... | collective-permute-start | bytes 196616 | tf_op jit(solution)/shard_map/ppermute | solution.py:315
  6.0 3.2 %collective-permute-done.1 = f32[128,128]{0,1:T(8,128)S(1)} collective-permute-done((f32[128,128]{0,1:T(8,128)S(1)}, f32[128,128]{0,1:T(8,128)S(1)}, u32[]{:S(2)}, u32[]{:S(2)}) %collective-permute-start.1) | collective-permute-done | bytes 65568 | tf_op jit(solution)/shard_map/ppermute | solution.py:315
  9.7 6.1 %collective-permute-start.4 = (f16[128,128]{1,0:T(8,128)(2,1)S(1)}, f16[128,128]{1,0:T(8,128)(2,1)S(1)}, u32[]{:S(2)}, u32[]{:S(2)}) collective-permute-start(f16[128,128]{1,0:T(8,128)(2,1)S(1)} %bitcast.78), channel_id=1, source_target_pairs={{0,20},{4,24},{8,28},{12,0},{16,4},{20,8},{24,12},{28,16},{1,21},{... | collective-permute-start | bytes 98312 | tf_op jit(solution)/shard_map/ppermute | solution.py:315
  15.9 2.0 %shard_map.119 = bf16[8,5,4,32,128]{4,3,2,1,0:T(8,128)(2,1)} custom-call(bf16[1,32,40,128]{3,2,1,0:T(8,128)(2,1)S(1)} %copy-done.3, bf16[1,32,40,128]{3,2,1,0:T(8,128)(2,1)S(1)} %copy-done.4, bf16[1,32,40,128]{3,2,1,0:T(8,128)(2,1)S(1)} %copy-done.5, bf16[1,32,40,128]{3,2,1,0:T(8,128)(2,1)S(1)} %copy-done, bf16[1,32,40,128]{3,2,1,0:T(8,128)(2,1)S(1)} %copy-done.1), custom_call_target="tpu_custom_call" | custom-call | tf_op jit(solution)/shard_map/pallas_call | solution.py:292
  17.8 4.9 %collective-permute-done.3 = f16[128,128]{1,0:T(8,128)(2,1)S(1)} collective-permute-done((f16[128,128]{1,0:T(8,128)(2,1)S(1)}, f16[128,128]{1,0:T(8,128)(2,1)S(1)}, u32[]{:S(2)}, u32[]{:S(2)}) %collective-permute-start.3) | collective-permute-done | bytes 32800 | tf_op jit(solution)/shard_map/ppermute | solution.py:315
  23.9 2.3 %collective-permute-start.6 = (f16[2,128,128]{2,1,0:T(8,128)(2,1)S(1)}, f16[2,128,128]{2,1,0:T(8,128)(2,1)S(1)}, u32[]{:S(2)}, u32[]{:S(2)}) collective-permute-start(f16[2,128,128]{2,1,0:T(8,128)(2,1)S(1)} %pad_maximum_fusion.3), channel_id=1, source_target_pairs={{0,28},{4,0},{8,4},{12,8},{16,12},{20,16},{24,20},{28,24},{1,29},{... | collective-permute-start | bytes 196616 | tf_op jit(solution)/shard_map/ppermute | solution.py:315
  26.2 2.5 %collective-permute-done.5 = f16[3,128,128]{2,1,0:T(8,128)(2,1)S(1)} collective-permute-done((f16[3,128,128]{2,1,0:T(8,128)(2,1)S(1)}, f16[3,128,128]{2,1,0:T(8,128)(2,1)S(1)}, u32[]{:S(2)}, u32[]{:S(2)}) %collective-permute-start.5) | collective-permute-done | bytes 98336 | tf_op jit(solution)/shard_map/ppermute | solution.py:315
  28.9 4.2 %all-to-all-start = ((bf16[8,5,4,32,128]{4,3,2,1,0:T(8,128)(2,1)}), bf16[8,5,4,32,128]{4,3,2,1,0:T(8,128)(2,1)S(1)}, u32[]{:S(2)}, u32[]{:S(2)}) async-start(bf16[8,5,4,32,128]{4,3,2,1,0:T(8,128)(2,1)} %shard_map.119), calls=%async_computation | async-start | bytes 2621440 | tf_op jit(solution)/shard_map/all_to_all | solution.py:367
  33.1 2.4 %collective-permute-start.7 = (f16[8,128,128]{2,1,0:T(8,128)(2,1)S(1)}, f16[8,128,128]{2,1,0:T(8,128)(2,1)S(1)}, u32[]{:S(2)}, u32[]{:S(2)}) collective-permute-start(f16[8,128,128]{2,1,0:T(8,128)(2,1)S(1)} %slice_dynamic-update-slice_fusion), channel_id=1, source_target_pairs={{0,128},{32,160},{64,192},{96,224},{128,0},{160,32},{192,64},{224,... | collective-permute-start | bytes 786440 | tf_op jit(solution)/shard_map/ppermute | solution.py:323
  35.5 5.6 %collective-permute-done.7 = f16[8,128,128]{2,1,0:T(8,128)(2,1)S(1)} collective-permute-done((f16[8,128,128]{2,1,0:T(8,128)(2,1)S(1)}, f16[8,128,128]{2,1,0:T(8,128)(2,1)S(1)}, u32[]{:S(2)}, u32[]{:S(2)}) %collective-permute-start.7) | collective-permute-done | bytes 262176 | tf_op jit(solution)/shard_map/ppermute | solution.py:323
  42.1 3.0 %collective-permute-start.10 = (f16[2,8,128,128]{3,2,1,0:T(8,128)(2,1)}, f16[2,8,128,128]{3,2,1,0:T(8,128)(2,1)}, u32[]{:S(2)}, u32[]{:S(2)}) collective-permute-start(f16[2,8,128,128]{3,2,1,0:T(8,128)(2,1)} %get-tuple-element.75), channel_id=1, source_target_pairs={{0,64},{32,96},{64,0},{96,32},{128,192},{160,224},{192,128},{224,1... | collective-permute-start | bytes 1572872 | tf_op jit(solution)/shard_map/ppermute | solution.py:319
  45.7 2.6 %collective-permute-start.9 = (f16[2,8,128,128]{3,2,1,0:T(8,128)(2,1)}, f16[2,8,128,128]{3,2,1,0:T(8,128)(2,1)}, u32[]{:S(2)}, u32[]{:S(2)}) collective-permute-start(f16[2,8,128,128]{3,2,1,0:T(8,128)(2,1)} %get-tuple-element.75), channel_id=1, source_target_pairs={{0,96},{32,0},{64,32},{96,64},{128,224},{160,128},{192,160},{224,1... | collective-permute-start | bytes 1572872 | tf_op jit(solution)/shard_map/ppermute | solution.py:319
  49.7 8.5 %collective-permute-done.10 = f16[2,8,128,128]{3,2,1,0:T(8,128)(2,1)} collective-permute-done((f16[2,8,128,128]{3,2,1,0:T(8,128)(2,1)}, f16[2,8,128,128]{3,2,1,0:T(8,128)(2,1)}, u32[]{:S(2)}, u32[]{:S(2)}) %collective-permute-start.10) | collective-permute-done | bytes 524320 | tf_op jit(solution)/shard_map/ppermute | solution.py:319
  58.2 2.1 %convert_element_type.67.refs_2_ = f32[2,8,128,128]{3,2,1,0:T(8,128)} convert(f16[2,8,128,128]{3,2,1,0:T(8,128)(2,1)} %collective-permute-done.10) | non-fusion elementwise | flops 262144 | bytes 1572864 | tf_op jit(solution)/shard_map/convert_element_type | solution.py:371
  60.3 3.5 %all-to-all-done.refs_1_ = bf16[8,5,4,32,128]{4,3,2,1,0:T(8,128)(2,1)S(1)} async-done(((bf16[8,5,4,32,128]{4,3,2,1,0:T(8,128)(2,1)}), bf16[8,5,4,32,128]{4,3,2,1,0:T(8,128)(2,1)S(1)}, u32[]{:S(2)}, u32[]{:S(2)}) %all-to-all-start) | async-done | bytes 1310752 | tf_op jit(solution)/shard_map/all_to_all | solution.py:367
  65.1 8.5 %shard_map.120 = (bf16[8,5,2,32,128]{4,3,2,1,0:T(8,128)(2,1)S(1)}, bf16[2,8,128,128]{3,2,1,0:T(8,128)(2,1)S(1)}, bf16[5,1024,128]{2,1,0:T(8,128)(2,1)S(1)}, bf16...) custom-call(s32[10]{0:T(128)S(1)} %pad_add_fusion.refs_0_, bf16[8,5,4,32,128]{4,3,2,1,0:T(8,128)(2,1)S(1)} %all-to-all-done.refs_1_, ...), custom_call_target="tpu_custom_call" | custom-call | flops 2000000000 | bytes 8000000 | tf_op jit(solution)/shard_map/pallas_call | solution.py:259
  74.8 3.1 %collective-permute-start.11 = (bf16[2,8,128,128]{3,2,1,0:T(8,128)(2,1)S(1)}, bf16[2,8,128,128]{3,2,1,0:T(8,128)(2,1)S(1)}, u32[]{:S(2)}, u32[]{:S(2)}) collective-permute-start(bf16[2,8,128,128]{3,2,1,0:T(8,128)(2,1)S(1)} %get-tuple-element.46), channel_id=1, source_target_pairs={{0,64},{32,96},{64,0},{96,32},{128,192},{160,224},{192,128},{224,1... | collective-permute-start | bytes 1572872 | tf_op jit(solution)/shard_map/ppermute | solution.py:319
  77.9 12.0 %shard_map.121 = (bf16[8,5,2,32,128]{4,3,2,1,0:T(8,128)(2,1)S(1)}, bf16[2,8,128,128]{3,2,1,0:T(8,128)(2,1)S(1)}, bf16[2,8,128,128]{3,2,1,0:T(8,128)(2,1)S(1)}, f32[5,1024,128]{2,1,0:T(8,128)S(1)}) custom-call(s32[10]{0:T(128)S(1)} %pad_add_fusion.refs_0_, bf16[8,5,4,32,128]{4,3,2,1,0:T(8,128)(2,1)S(1)} %all-to-all-done.refs_1_, ...), custom_call_target="tpu_custom_call" | custom-call | flops 4000000000 | bytes 8000000 | tf_op jit(solution)/shard_map/pallas_call | solution.py:259
  90.6 2.7 %collective-permute-start.12 = (bf16[2,8,128,128]{3,2,1,0:T(8,128)(2,1)S(1)}, bf16[2,8,128,128]{3,2,1,0:T(8,128)(2,1)S(1)}, u32[]{:S(2)}, u32[]{:S(2)}) collective-permute-start(bf16[2,8,128,128]{3,2,1,0:T(8,128)(2,1)S(1)} %get-tuple-element.50), channel_id=1, source_target_pairs={{0,96},{32,0},{64,32},{96,64},{128,224},{160,128},{192,160},{224,1... | collective-permute-start | bytes 1572872 | tf_op jit(solution)/shard_map/ppermute | solution.py:319
  93.3 9.4 %shard_map.122 = (bf16[8,5,2,32,128]{4,3,2,1,0:T(8,128)(2,1)}, bf16[8,5,2,32,128]{4,3,2,1,0:T(8,128)(2,1)}, f32[2,8,128,128]{3,2,1,0:T(8,128)S(1)}) custom-call(s32[10]{0:T(128)S(1)} %pad_add_fusion.refs_0_, bf16[8,5,4,32,128]{4,3,2,1,0:T(8,128)(2,1)S(1)} %all-to-all-done.refs_1_, f32[2,8,128,128]{3,2,1,0:T(8,128)S(1)} %get-tuple-element.76.refs_2_, ...), custom_call_target="tpu_custom_call" | custom-call | flops 2000000000 | bytes 8000000 | tf_op jit(solution)/shard_map/pallas_call | solution.py:259
  102.9 2.4 %collective-permute-start.14 = (bf16[8,128,128]{2,1,0:T(8,128)(2,1)S(1)}, bf16[8,128,128]{2,1,0:T(8,128)(2,1)S(1)}, u32[]{:S(2)}, u32[]{:S(2)}) collective-permute-start(bf16[8,128,128]{2,1,0:T(8,128)(2,1)S(1)} %fusion.4), channel_id=1, source_target_pairs={{0,128},{32,160},{64,192},{96,224},{128,0},{160,32},{192,64},{224,... | collective-permute-start | bytes 786440 | tf_op jit(solution)/shard_map/ppermute | solution.py:323
  105.3 3.5 %all-to-all-start.1 = ((bf16[8,5,2,32,128]{4,3,2,1,0:T(8,128)(2,1)}), bf16[8,5,2,32,128]{4,3,2,1,0:T(8,128)(2,1)S(1)}, u32[]{:S(2)}, u32[]{:S(2)}) async-start(bf16[8,5,2,32,128]{4,3,2,1,0:T(8,128)(2,1)} %get-tuple-element.47), calls=%async_computation.1 | async-start | bytes 1310720 | tf_op jit(solution)/shard_map/all_to_all | solution.py:378
  108.8 2.0 %collective-permute-done.14 = bf16[8,128,128]{2,1,0:T(8,128)(2,1)S(1)} collective-permute-done((bf16[8,128,128]{2,1,0:T(8,128)(2,1)S(1)}, bf16[8,128,128]{2,1,0:T(8,128)(2,1)S(1)}, u32[]{:S(2)}, u32[]{:S(2)}) %collective-permute-start.14) | collective-permute-done | bytes 262176 | tf_op jit(solution)/shard_map/ppermute | solution.py:323
  113.2 8.8 %collective-permute-done.16 = bf16[2,128,128]{2,1,0:T(8,128)(2,1)S(1)} collective-permute-done((bf16[2,128,128]{2,1,0:T(8,128)(2,1)S(1)}, bf16[2,128,128]{2,1,0:T(8,128)(2,1)S(1)}, u32[]{:S(2)}, u32[]{:S(2)}) %collective-permute-start.16) | collective-permute-done | bytes 65568 | tf_op jit(solution)/shard_map/ppermute | solution.py:315
  123.3 3.9 %collective-permute-start.17 = (bf16[128,128]{1,0:T(8,128)(2,1)S(1)}, bf16[128,128]{1,0:T(8,128)(2,1)S(1)}, u32[]{:S(2)}, u32[]{:S(2)}) collective-permute-start(bf16[128,128]{1,0:T(8,128)(2,1)S(1)} %get-tuple-element.74), channel_id=1, source_target_pairs={{0,20},{4,24},{8,28},{12,0},{16,4},{20,8},{24,12},{28,16},{1,21},{... | collective-permute-start | bytes 98312 | tf_op jit(solution)/shard_map/ppermute | solution.py:315
  130.5 3.7 %collective-permute-done.18 = bf16[128,128]{1,0:T(8,128)(2,1)S(1)} collective-permute-done((bf16[128,128]{1,0:T(8,128)(2,1)S(1)}, bf16[128,128]{1,0:T(8,128)(2,1)S(1)}, u32[]{:S(2)}, u32[]{:S(2)}) %collective-permute-start.18) | collective-permute-done | bytes 32800 | tf_op jit(solution)/shard_map/ppermute | solution.py:315
  134.2 5.3 %all-to-all-start.2 = ((bf16[8,5,2,32,128]{4,3,2,1,0:T(8,128)(2,1)}), bf16[8,5,2,32,128]{4,3,2,1,0:T(8,128)(2,1)S(1)}, u32[]{:S(2)}, u32[]{:S(2)}) async-start(bf16[8,5,2,32,128]{4,3,2,1,0:T(8,128)(2,1)} %get-tuple-element.53), calls=%async_computation.2 | async-start | bytes 1310720 | tf_op jit(solution)/shard_map/all_to_all | solution.py:382
  140.2 1.9 %collective-permute-start.20 = (f32[128,128]{0,1:T(8,128)S(1)}, f32[128,128]{0,1:T(8,128)S(1)}, u32[]{:S(2)}, u32[]{:S(2)}) collective-permute-start(f32[128,128]{0,1:T(8,128)S(1)} %fusion.14), channel_id=1, source_target_pairs={{0,2},{1,3},{2,0},{3,1},{4,6},{5,7},{6,4},{7,5},{8,10},{9,11},{10,... | collective-permute-start | bytes 196616 | tf_op jit(solution)/shard_map/ppermute | solution.py:315
  142.4 3.3 %collective-permute-done.20 = f32[128,128]{0,1:T(8,128)S(1)} collective-permute-done((f32[128,128]{0,1:T(8,128)S(1)}, f32[128,128]{0,1:T(8,128)S(1)}, u32[]{:S(2)}, u32[]{:S(2)}) %collective-permute-start.20) | collective-permute-done | bytes 65568 | tf_op jit(solution)/shard_map/ppermute | solution.py:315
  146.2 2.1 %convolution_convert_fusion = bf16[32,128,128]{2,0,1:T(8,128)(2,1)S(1)} fusion(f32[1,16384]{1,0:T(1,128)S(1)} %bitcast.85, f32[1,16384]{1,0:T(1,128)S(1)} %bitcast.86, f32[1,16384]{1,0:T(1,128)S(1)} %bitcast.87, f32[1,16384]{1,0:T(1,128)S(1)} %bitcast.84, f32[4,32]{1,0:T(4,128)S(1)} %gather_fusion, pred[4]{0:T(512)(128)(4,1)S(1)} %compare_and_fusion), kind=kOutput, calls=%fused_computation.1 | convolution fusion | flops 25886848 | bytes 1311236 | tf_op jit(solution)/shard_map/dot_general | solution.py:390
  151.1 3.1 %all-to-all-done.2.x_ref = bf16[8,5,2,32,128]{4,3,2,1,0:T(8,128)(2,1)S(1)} async-done(((bf16[8,5,2,32,128]{4,3,2,1,0:T(8,128)(2,1)}), bf16[8,5,2,32,128]{4,3,2,1,0:T(8,128)(2,1)S(1)}, u32[]{:S(2)}, u32[]{:S(2)}) %all-to-all-start.2) | async-done | bytes 655392 | tf_op jit(solution)/shard_map/all_to_all | solution.py:382
  (86 shorter events, 21.3 us)
Async XLA Ops:
  0.7 15.1 %copy-start = (bf16[1,32,40,128]{3,2,1,0:T(8,128)(2,1)S(1)}, bf16[1,32,40,128]{3,2,1,0:T(8,128)(2,1)}, u32[]{:S(2)}) copy-start(bf16[1,32,40,128]{3,2,1,0:T(8,128)(2,1)} %g_ref.3) | copy-start | bytes 983044
  0.7 15.1 %copy-start.1 = (bf16[1,32,40,128]{3,2,1,0:T(8,128)(2,1)S(1)}, bf16[1,32,40,128]{3,2,1,0:T(8,128)(2,1)}, u32[]{:S(2)}) copy-start(bf16[1,32,40,128]{3,2,1,0:T(8,128)(2,1)} %c_ref.3) | copy-start | bytes 983044
  0.7 15.1 %copy-start.3 = (bf16[1,32,40,128]{3,2,1,0:T(8,128)(2,1)S(1)}, bf16[1,32,40,128]{3,2,1,0:T(8,128)(2,1)}, u32[]{:S(2)}) copy-start(bf16[1,32,40,128]{3,2,1,0:T(8,128)(2,1)} %q_ref.1) | copy-start | bytes 983044
  0.7 15.1 %copy-start.4 = (bf16[1,32,40,128]{3,2,1,0:T(8,128)(2,1)S(1)}, bf16[1,32,40,128]{3,2,1,0:T(8,128)(2,1)}, u32[]{:S(2)}) copy-start(bf16[1,32,40,128]{3,2,1,0:T(8,128)(2,1)} %k_ref.1) | copy-start | bytes 983044
  0.7 15.1 %copy-start.5 = (bf16[1,32,40,128]{3,2,1,0:T(8,128)(2,1)S(1)}, bf16[1,32,40,128]{3,2,1,0:T(8,128)(2,1)}, u32[]{:S(2)}) copy-start(bf16[1,32,40,128]{3,2,1,0:T(8,128)(2,1)} %v_ref.1) | copy-start | bytes 983044
  3.1 2.9 %collective-permute-start.2 = (f32[128,128]{0,1:T(8,128)S(1)}, f32[128,128]{0,1:T(8,128)S(1)}, u32[]{:S(2)}, u32[]{:S(2)}) collective-permute-start(f32[128,128]{0,1:T(8,128)S(1)} %bitcast.90), channel_id=1, source_target_pairs={{0,3},{1,0},{2,1},{3,2},{4,7},{5,4},{6,5},{7,6},{8,11},{9,8},{10,9... | collective-permute-start | bytes 196616 | tf_op jit(solution)/shard_map/ppermute | solution.py:315
  3.3 6.0 %collective-permute-start.1 = (f32[128,128]{0,1:T(8,128)S(1)}, f32[128,128]{0,1:T(8,128)S(1)}, u32[]{:S(2)}, u32[]{:S(2)}) collective-permute-start(f32[128,128]{0,1:T(8,128)S(1)} %bitcast.91), channel_id=1, source_target_pairs={{0,2},{1,3},{2,0},{3,1},{4,6},{5,7},{6,4},{7,5},{8,10},{9,11},{10,... | collective-permute-start | bytes 196616 | tf_op jit(solution)/shard_map/ppermute | solution.py:315
  5.6 4.1 %collective-permute-start = (f32[128,128]{0,1:T(8,128)S(1)}, f32[128,128]{0,1:T(8,128)S(1)}, u32[]{:S(2)}, u32[]{:S(2)}) collective-permute-start(f32[128,128]{0,1:T(8,128)S(1)} %bitcast.92), channel_id=1, source_target_pairs={{0,1},{1,2},{2,3},{3,0},{4,5},{5,6},{6,7},{7,4},{8,9},{9,10},{10,1... | collective-permute-start | bytes 196616 | tf_op jit(solution)/shard_map/ppermute | solution.py:315
  9.7 8.1 %collective-permute-start.4 = (f16[128,128]{1,0:T(8,128)(2,1)S(1)}, f16[128,128]{1,0:T(8,128)(2,1)S(1)}, u32[]{:S(2)}, u32[]{:S(2)}) collective-permute-start(f16[128,128]{1,0:T(8,128)(2,1)S(1)} %bitcast.78), channel_id=1, source_target_pairs={{0,20},{4,24},{8,28},{12,0},{16,4},{20,8},{24,12},{28,16},{1,21},{... | collective-permute-start | bytes 98312 | tf_op jit(solution)/shard_map/ppermute | solution.py:315
  15.8 7.0 %collective-permute-start.3 = (f16[128,128]{1,0:T(8,128)(2,1)S(1)}, f16[128,128]{1,0:T(8,128)(2,1)S(1)}, u32[]{:S(2)}, u32[]{:S(2)}) collective-permute-start(f16[128,128]{1,0:T(8,128)(2,1)S(1)} %bitcast.79), channel_id=1, source_target_pairs={{0,12},{4,16},{8,20},{12,24},{16,28},{20,0},{24,4},{28,8},{1,13},{... | collective-permute-start | bytes 98312 | tf_op jit(solution)/shard_map/ppermute | solution.py:315
  22.8 5.9 %collective-permute-start.5 = (f16[3,128,128]{2,1,0:T(8,128)(2,1)S(1)}, f16[3,128,128]{2,1,0:T(8,128)(2,1)S(1)}, u32[]{:S(2)}, u32[]{:S(2)}) collective-permute-start(f16[3,128,128]{2,1,0:T(8,128)(2,1)S(1)} %pad_maximum_fusion.1), channel_id=1, source_target_pairs={{0,4},{4,8},{8,12},{12,16},{16,20},{20,24},{24,28},{28,0},{1,5},{5... | collective-permute-start | bytes 294920 | tf_op jit(solution)/shard_map/ppermute | solution.py:315
  23.9 4.8 %collective-permute-start.6 = (f16[2,128,128]{2,1,0:T(8,128)(2,1)S(1)}, f16[2,128,128]{2,1,0:T(8,128)(2,1)S(1)}, u32[]{:S(2)}, u32[]{:S(2)}) collective-permute-start(f16[2,128,128]{2,1,0:T(8,128)(2,1)S(1)} %pad_maximum_fusion.3), channel_id=1, source_target_pairs={{0,28},{4,0},{8,4},{12,8},{16,12},{20,16},{24,20},{28,24},{1,29},{... | collective-permute-start | bytes 196616 | tf_op jit(solution)/shard_map/ppermute | solution.py:315
  28.9 34.9 %all-to-all-start = ((bf16[8,5,4,32,128]{4,3,2,1,0:T(8,128)(2,1)}), bf16[8,5,4,32,128]{4,3,2,1,0:T(8,128)(2,1)S(1)}, u32[]{:S(2)}, u32[]{:S(2)}) async-start(bf16[8,5,4,32,128]{4,3,2,1,0:T(8,128)(2,1)} %shard_map.119), calls=%async_computation | async-start | bytes 2621440 | tf_op jit(solution)/shard_map/all_to_all | solution.py:367
  33.1 15.2 %copy-start.7 = (s32[8]{0:T(128)S(1)}, s32[8]{0:T(128)}, u32[]{:S(2)}) copy-start(s32[8]{0:T(128)} %param.15) | copy-start | bytes 100
  33.1 8.0 %collective-permute-start.7 = (f16[8,128,128]{2,1,0:T(8,128)(2,1)S(1)}, f16[8,128,128]{2,1,0:T(8,128)(2,1)S(1)}, u32[]{:S(2)}, u32[]{:S(2)}) collective-permute-start(f16[8,128,128]{2,1,0:T(8,128)(2,1)S(1)} %slice_dynamic-update-slice_fusion), channel_id=1, source_target_pairs={{0,128},{32,160},{64,192},{96,224},{128,0},{160,32},{192,64},{224,... | collective-permute-start | bytes 786440 | tf_op jit(solution)/shard_map/ppermute | solution.py:323
  42.1 16.1 %collective-permute-start.10 = (f16[2,8,128,128]{3,2,1,0:T(8,128)(2,1)}, f16[2,8,128,128]{3,2,1,0:T(8,128)(2,1)}, u32[]{:S(2)}, u32[]{:S(2)}) collective-permute-start(f16[2,8,128,128]{3,2,1,0:T(8,128)(2,1)} %get-tuple-element.75), channel_id=1, source_target_pairs={{0,64},{32,96},{64,0},{96,32},{128,192},{160,224},{192,128},{224,1... | collective-permute-start | bytes 1572872 | tf_op jit(solution)/shard_map/ppermute | solution.py:319
  45.1 28.4 %collective-permute-start.8 = (f16[2,8,128,128]{3,2,1,0:T(8,128)(2,1)}, f16[2,8,128,128]{3,2,1,0:T(8,128)(2,1)S(1)}, u32[]{:S(2)}, u32[]{:S(2)}) collective-permute-start(f16[2,8,128,128]{3,2,1,0:T(8,128)(2,1)} %get-tuple-element.75), channel_id=1, source_target_pairs={{0,32},{32,64},{64,96},{96,0},{128,160},{160,192},{192,224},{224,1... | collective-permute-start | bytes 1572872 | tf_op jit(solution)/shard_map/ppermute | solution.py:319
  45.7 27.9 %collective-permute-start.9 = (f16[2,8,128,128]{3,2,1,0:T(8,128)(2,1)}, f16[2,8,128,128]{3,2,1,0:T(8,128)(2,1)}, u32[]{:S(2)}, u32[]{:S(2)}) collective-permute-start(f16[2,8,128,128]{3,2,1,0:T(8,128)(2,1)} %get-tuple-element.75), channel_id=1, source_target_pairs={{0,96},{32,0},{64,32},{96,64},{128,224},{160,128},{192,160},{224,1... | collective-permute-start | bytes 1572872 | tf_op jit(solution)/shard_map/ppermute | solution.py:319
  74.8 18.5 %collective-permute-start.11 = (bf16[2,8,128,128]{3,2,1,0:T(8,128)(2,1)S(1)}, bf16[2,8,128,128]{3,2,1,0:T(8,128)(2,1)S(1)}, u32[]{:S(2)}, u32[]{:S(2)}) collective-permute-start(bf16[2,8,128,128]{3,2,1,0:T(8,128)(2,1)S(1)} %get-tuple-element.46), channel_id=1, source_target_pairs={{0,64},{32,96},{64,0},{96,32},{128,192},{160,224},{192,128},{224,1... | collective-permute-start | bytes 1572872 | tf_op jit(solution)/shard_map/ppermute | solution.py:319
  89.9 12.8 %collective-permute-start.13 = (bf16[2,8,128,128]{3,2,1,0:T(8,128)(2,1)S(1)}, bf16[2,8,128,128]{3,2,1,0:T(8,128)(2,1)S(1)}, u32[]{:S(2)}, u32[]{:S(2)}) collective-permute-start(bf16[2,8,128,128]{3,2,1,0:T(8,128)(2,1)S(1)} %get-tuple-element.51), channel_id=1, source_target_pairs={{0,32},{32,64},{64,96},{96,0},{128,160},{160,192},{192,224},{224,1... | collective-permute-start | bytes 1572872 | tf_op jit(solution)/shard_map/ppermute | solution.py:319
  90.6 12.1 %collective-permute-start.12 = (bf16[2,8,128,128]{3,2,1,0:T(8,128)(2,1)S(1)}, bf16[2,8,128,128]{3,2,1,0:T(8,128)(2,1)S(1)}, u32[]{:S(2)}, u32[]{:S(2)}) collective-permute-start(bf16[2,8,128,128]{3,2,1,0:T(8,128)(2,1)S(1)} %get-tuple-element.50), channel_id=1, source_target_pairs={{0,96},{32,0},{64,32},{96,64},{128,224},{160,128},{192,160},{224,1... | collective-permute-start | bytes 1572872 | tf_op jit(solution)/shard_map/ppermute | solution.py:319
  102.9 8.0 %collective-permute-start.14 = (bf16[8,128,128]{2,1,0:T(8,128)(2,1)S(1)}, bf16[8,128,128]{2,1,0:T(8,128)(2,1)S(1)}, u32[]{:S(2)}, u32[]{:S(2)}) collective-permute-start(bf16[8,128,128]{2,1,0:T(8,128)(2,1)S(1)} %fusion.4), channel_id=1, source_target_pairs={{0,128},{32,160},{64,192},{96,224},{128,0},{160,32},{192,64},{224,... | collective-permute-start | bytes 786440 | tf_op jit(solution)/shard_map/ppermute | solution.py:323
  105.3 28.9 %all-to-all-start.1 = ((bf16[8,5,2,32,128]{4,3,2,1,0:T(8,128)(2,1)}), bf16[8,5,2,32,128]{4,3,2,1,0:T(8,128)(2,1)S(1)}, u32[]{:S(2)}, u32[]{:S(2)}) async-start(bf16[8,5,2,32,128]{4,3,2,1,0:T(8,128)(2,1)} %get-tuple-element.47), calls=%async_computation.1 | async-start | bytes 1310720 | tf_op jit(solution)/shard_map/all_to_all | solution.py:378
  111.0 28.4 %copy-start.6 = (bf16[32,4]{0,1:T(4,128)(2,1)S(1)}, bf16[32,4]{0,1:T(4,128)(2,1)}, u32[]{:S(2)}) copy-start(bf16[32,4]{0,1:T(4,128)(2,1)} %param.14) | copy-start | bytes 772
  111.0 12.2 %collective-permute-start.15 = (bf16[3,128,128]{2,1,0:T(8,128)(2,1)S(1)}, bf16[3,128,128]{2,1,0:T(8,128)(2,1)S(1)}, u32[]{:S(2)}, u32[]{:S(2)}) collective-permute-start(bf16[3,128,128]{2,1,0:T(8,128)(2,1)S(1)} %pad_maximum_fusion.2), channel_id=1, source_target_pairs={{0,28},{4,0},{8,4},{12,8},{16,12},{20,16},{24,20},{28,24},{1,29},{... | collective-permute-start | bytes 294920 | tf_op jit(solution)/shard_map/ppermute | solution.py:315
  112.3 9.8 %collective-permute-start.16 = (bf16[2,128,128]{2,1,0:T(8,128)(2,1)S(1)}, bf16[2,128,128]{2,1,0:T(8,128)(2,1)S(1)}, u32[]{:S(2)}, u32[]{:S(2)}) collective-permute-start(bf16[2,128,128]{2,1,0:T(8,128)(2,1)S(1)} %pad_maximum_fusion.4), channel_id=1, source_target_pairs={{0,4},{4,8},{8,12},{12,16},{16,20},{20,24},{24,28},{28,0},{1,5},{5... | collective-permute-start | bytes 196616 | tf_op jit(solution)/shard_map/ppermute | solution.py:315
  123.3 7.2 %collective-permute-start.17 = (bf16[128,128]{1,0:T(8,128)(2,1)S(1)}, bf16[128,128]{1,0:T(8,128)(2,1)S(1)}, u32[]{:S(2)}, u32[]{:S(2)}) collective-permute-start(bf16[128,128]{1,0:T(8,128)(2,1)S(1)} %get-tuple-element.74), channel_id=1, source_target_pairs={{0,20},{4,24},{8,28},{12,0},{16,4},{20,8},{24,12},{28,16},{1,21},{... | collective-permute-start | bytes 98312 | tf_op jit(solution)/shard_map/ppermute | solution.py:315
  127.2 6.9 %collective-permute-start.18 = (bf16[128,128]{1,0:T(8,128)(2,1)S(1)}, bf16[128,128]{1,0:T(8,128)(2,1)S(1)}, u32[]{:S(2)}, u32[]{:S(2)}) collective-permute-start(bf16[128,128]{1,0:T(8,128)(2,1)S(1)} %get-tuple-element.73), channel_id=1, source_target_pairs={{0,12},{4,16},{8,20},{12,24},{16,28},{20,0},{24,4},{28,8},{1,13},{... | collective-permute-start | bytes 98312 | tf_op jit(solution)/shard_map/ppermute | solution.py:315
  134.2 20.0 %all-to-all-start.2 = ((bf16[8,5,2,32,128]{4,3,2,1,0:T(8,128)(2,1)}), bf16[8,5,2,32,128]{4,3,2,1,0:T(8,128)(2,1)S(1)}, u32[]{:S(2)}, u32[]{:S(2)}) async-start(bf16[8,5,2,32,128]{4,3,2,1,0:T(8,128)(2,1)} %get-tuple-element.53), calls=%async_computation.2 | async-start | bytes 1310720 | tf_op jit(solution)/shard_map/all_to_all | solution.py:382
  140.1 2.2 %collective-permute-start.21 = (f32[128,128]{0,1:T(8,128)S(1)}, f32[128,128]{0,1:T(8,128)S(1)}, u32[]{:S(2)}, u32[]{:S(2)}) collective-permute-start(f32[128,128]{0,1:T(8,128)S(1)} %fusion.14), channel_id=1, source_target_pairs={{0,3},{1,0},{2,1},{3,2},{4,7},{5,4},{6,5},{7,6},{8,11},{9,8},{10,9... | collective-permute-start | bytes 196616 | tf_op jit(solution)/shard_map/ppermute | solution.py:315
  140.2 5.5 %collective-permute-start.20 = (f32[128,128]{0,1:T(8,128)S(1)}, f32[128,128]{0,1:T(8,128)S(1)}, u32[]{:S(2)}, u32[]{:S(2)}) collective-permute-start(f32[128,128]{0,1:T(8,128)S(1)} %fusion.14), channel_id=1, source_target_pairs={{0,2},{1,3},{2,0},{3,1},{4,6},{5,7},{6,4},{7,5},{8,10},{9,11},{10,... | collective-permute-start | bytes 196616 | tf_op jit(solution)/shard_map/ppermute | solution.py:315
  142.0 4.1 %collective-permute-start.19 = (f32[128,128]{0,1:T(8,128)S(1)}, f32[128,128]{0,1:T(8,128)S(1)}, u32[]{:S(2)}, u32[]{:S(2)}) collective-permute-start(f32[128,128]{0,1:T(8,128)S(1)} %fusion.14), channel_id=1, source_target_pairs={{0,1},{1,2},{2,3},{3,0},{4,5},{5,6},{6,7},{7,4},{8,9},{9,10},{10,1... | collective-permute-start | bytes 196616 | tf_op jit(solution)/shard_map/ppermute | solution.py:315
  (1 other events, 1.2 us)
